TPU v7x, 512 devices: a whole 4x8x8 slice. The times are simulated.
512 devices in a mesh: fsdp: 32 (over z_hi, x, core), sp: 16 (over z_lo, y).
Axes of the slice: x: 4, y: 8, z: 8 (z_hi: 4, z_lo: 2; z = z_hi * 2 + z_lo), core: 2. Of those that a mesh axis runs over, the one named last changes fastest.
Arguments:
- query: bfloat16 [65536, 2048], P(('fsdp', 'sp')), may hold values from -6 to 6
- projected_key_rows: bfloat16 [65536, 2048], P(('fsdp', 'sp')), may hold values from -6 to 6
- value: bfloat16 [65536, 2048], P(('fsdp', 'sp')), may hold values from -6 to 6
- blocks: int32 [32, 16, 6], P('fsdp'), may hold values from 0 to 15, as said below
- frozen_output_weight: bfloat16 [2048, 2048], P('fsdp'), may hold values from -0.125 to 0.125
- adapter_down_weight: bfloat16 [2048, 64], P('fsdp'), may hold values from -0.125 to 0.125
- adapter_up_weight_transposed: bfloat16 [2048, 64], P('fsdp'), may hold values from -0.75 to 0.75
- cotangent: bfloat16 [65536, 2048], P(('fsdp', 'sp')), may hold values from -24 to 24
Outputs:
- mixed: bfloat16 [65536, 2048], P(('fsdp', 'sp'))
- grad_query: bfloat16 [65536, 2048], P(('fsdp', 'sp'))
- grad_key: bfloat16 [65536, 2048], P(('fsdp', 'sp'))
- grad_value: bfloat16 [65536, 2048], P(('fsdp', 'sp'))
- grad_down: float32 [2048, 64], P('fsdp')
- grad_up: float32 [2048, 64], P('fsdp')
Inputs may be any that keep to these rules, and one draw needn't show every extreme that they name: Entry 1 of each list is the query block itself, entries 0 and 2 its neighbours (wrapping at the ends), entry 3 one block common to all query blocks of the sequence, the rest any blocks.
All inputs are finite; a program needn't handle non-finite values.
Results may differ from a plain program's by a relative error of at most 0.0081.
Values may be sent and summed in bfloat16 or wider, within the bound.
A program may use at most 128 MiB of HBM per device.

v0:
```python
import math

import jax
import jax.numpy as jnp
from jax import lax
from jax.sharding import PartitionSpec as P

MODEL_WIDTH = 2048
HEADS = 16
BLOCK = 128
KEY_BLOCKS = 6
ADAPTER_RANK = 64


def gather_lists(key_blocks, value_blocks, lists_group):
    groups = lists_group.shape[0]
    listed = lists_group.reshape(-1)
    keys_gathered = jnp.take(key_blocks, listed, axis=0)
    values_gathered = jnp.take(value_blocks, listed, axis=0)
    keys_gathered = keys_gathered.reshape(
        groups, -1, keys_gathered.shape[2], keys_gathered.shape[3]
    )
    values_gathered = values_gathered.reshape(
        groups, -1, values_gathered.shape[2], values_gathered.shape[3]
    )
    return (keys_gathered, values_gathered)


def block_probs(query_group, keys_gathered, scaling):
    scores = (
        jnp.einsum(
            "gqhd,gkhd->ghqk", query_group, keys_gathered, preferred_element_type=jnp.float32
        )
        * scaling
    )
    highest = jnp.max(scores, axis=-1, keepdims=True)
    raised = jnp.exp(scores - highest)
    probs = raised / jnp.sum(raised, axis=-1, keepdims=True)
    return (probs, probs.astype(jnp.bfloat16))


def forward_group(query_group, key_blocks, value_blocks, lists_group, scaling):
    keys_gathered, values_gathered = gather_lists(key_blocks, value_blocks, lists_group)
    probs, weights = block_probs(query_group, keys_gathered, scaling)
    return jnp.einsum(
        "ghqk,gkhd->gqhd", weights, values_gathered, preferred_element_type=jnp.float32
    ).astype(jnp.bfloat16)


def backward_group(query_group, key_blocks, value_blocks, lists_group, grad_group, scaling):
    keys_gathered, values_gathered = gather_lists(key_blocks, value_blocks, lists_group)
    probs, weights = block_probs(query_group, keys_gathered, scaling)
    dweights = jnp.einsum(
        "gqhd,gkhd->ghqk", grad_group, values_gathered, preferred_element_type=jnp.float32
    )
    correction = jnp.sum(probs * dweights, axis=-1, keepdims=True)
    dscores = (probs * (dweights - correction) * scaling).astype(jnp.bfloat16)
    grad_query = jnp.einsum(
        "ghqk,gkhd->gqhd", dscores, keys_gathered, preferred_element_type=jnp.float32
    ).astype(jnp.bfloat16)
    key_terms = jnp.einsum(
        "ghqk,gqhd->gkhd", dscores, query_group, preferred_element_type=jnp.float32
    )
    value_terms = jnp.einsum(
        "ghqk,gqhd->gkhd", weights, grad_group, preferred_element_type=jnp.float32
    )
    listed = lists_group.reshape(-1)
    total_blocks = key_blocks.shape[0]
    one_hot = (listed[:, None] == jnp.arange(total_blocks, dtype=jnp.int32)[None, :]).astype(
        jnp.float32
    )
    entries = listed.shape[0]
    key_add = jnp.einsum(
        "in,ij->nj", one_hot, key_terms.reshape(entries, -1), precision=lax.Precision.HIGHEST
    )
    value_add = jnp.einsum(
        "in,ij->nj", one_hot, value_terms.reshape(entries, -1), precision=lax.Precision.HIGHEST
    )
    return (grad_query, key_add, value_add)


def shards(
    query,
    projected_key_rows,
    value,
    blocks,
    frozen_output_weight,
    adapter_down_weight,
    adapter_up_weight_transposed,
    cotangent,
):
    span = lax.axis_size("sp")
    full_out, full_down, full_up = (
        lax.all_gather(frozen_output_weight, "fsdp", axis=0, tiled=True),
        lax.all_gather(adapter_down_weight, "fsdp", axis=0, tiled=True),
        lax.all_gather(adapter_up_weight_transposed, "fsdp", axis=0, tiled=True),
    )
    heads_query, heads_key, heads_value = (
        lax.all_to_all(query, "sp", split_axis=1, concat_axis=0, tiled=True),
        lax.all_to_all(projected_key_rows, "sp", split_axis=1, concat_axis=0, tiled=True),
        lax.all_to_all(value, "sp", split_axis=1, concat_axis=0, tiled=True),
    )
    length = heads_query.shape[0]
    local_width = heads_query.shape[1]
    head_dim = MODEL_WIDTH // HEADS
    local_heads = local_width // head_dim
    scaling = 1.0 / math.sqrt(head_dim)
    block_count = length // BLOCK
    group_size = 4
    group_count = block_count // group_size
    query_groups = heads_query.reshape(group_count, group_size, BLOCK, local_heads, head_dim)
    key_blocks = heads_key.reshape(block_count, BLOCK, local_heads, head_dim)
    value_blocks = heads_value.reshape(block_count, BLOCK, local_heads, head_dim)
    list_groups = blocks[0].reshape(group_count, group_size, KEY_BLOCKS)
    context_groups = lax.map(
        lambda items: forward_group(items[0], key_blocks, value_blocks, items[1], scaling),
        (query_groups, list_groups),
    )
    context_heads = context_groups.reshape(length, local_width)
    attended_context = lax.all_to_all(context_heads, "sp", split_axis=0, concat_axis=1, tiled=True)
    reduced_rank_output = jnp.dot(
        attended_context, full_down, preferred_element_type=jnp.float32
    ).astype(jnp.bfloat16)
    mixed = (
        jnp.dot(attended_context, full_out, preferred_element_type=jnp.float32)
        + jnp.einsum("tr,dr->td", reduced_rank_output, full_up, preferred_element_type=jnp.float32)
    ).astype(jnp.bfloat16)
    reduced_gradient = jnp.dot(cotangent, full_up, preferred_element_type=jnp.float32).astype(
        jnp.bfloat16
    )
    attended_context_gradient = (
        jnp.einsum("td,ed->te", cotangent, full_out, preferred_element_type=jnp.float32)
        + jnp.einsum("tr,er->te", reduced_gradient, full_down, preferred_element_type=jnp.float32)
    ).astype(jnp.bfloat16)
    grad_heads = lax.all_to_all(
        attended_context_gradient, "sp", split_axis=1, concat_axis=0, tiled=True
    )
    token_total = query.shape[0] * span * lax.axis_size("fsdp")
    normal_factor = 1.0 / math.sqrt(token_total)
    partial_down = (
        jnp.einsum(
            "td,tr->dr", attended_context, reduced_gradient, preferred_element_type=jnp.float32
        )
        * normal_factor
    )
    partial_up = (
        jnp.einsum("td,tr->dr", cotangent, reduced_rank_output, preferred_element_type=jnp.float32)
        * normal_factor
    )
    summed_down, summed_up = lax.psum((partial_down, partial_up), "sp")
    grad_down, grad_up = (
        lax.psum_scatter(summed_down.reshape(-1), "fsdp", scatter_dimension=0, tiled=True),
        lax.psum_scatter(summed_up.reshape(-1), "fsdp", scatter_dimension=0, tiled=True),
    )
    grad_down = grad_down.reshape(-1, ADAPTER_RANK)
    grad_up = grad_up.reshape(-1, ADAPTER_RANK)
    grad_groups = grad_heads.reshape(group_count, group_size, BLOCK, local_heads, head_dim)
    block_size = BLOCK * local_width
    start_carry = (
        jnp.zeros((block_count, block_size), jnp.float32),
        jnp.zeros((block_count, block_size), jnp.float32),
    )

    def backward_step(carry, items):
        grad_query, key_add, value_add = backward_group(
            items[0], key_blocks, value_blocks, items[1], items[2], scaling
        )
        return ((carry[0] + key_add, carry[1] + value_add), grad_query)

    totals, query_grads = lax.scan(
        backward_step, start_carry, (query_groups, list_groups, grad_groups)
    )
    query_heads = query_grads.reshape(length, local_width)
    key_heads = totals[0].reshape(length, local_width).astype(jnp.bfloat16)
    value_heads = totals[1].reshape(length, local_width).astype(jnp.bfloat16)
    grad_query, grad_key, grad_value = (
        lax.all_to_all(query_heads, "sp", split_axis=0, concat_axis=1, tiled=True),
        lax.all_to_all(key_heads, "sp", split_axis=0, concat_axis=1, tiled=True),
        lax.all_to_all(value_heads, "sp", split_axis=0, concat_axis=1, tiled=True),
    )
    return (mixed, grad_query, grad_key, grad_value, grad_down, grad_up)


def solution(mesh):
    in_specs = (
        P(("fsdp", "sp"), None),
        P(("fsdp", "sp"), None),
        P(("fsdp", "sp"), None),
        P("fsdp", None, None),
        P("fsdp", None),
        P("fsdp", None),
        P("fsdp", None),
        P(("fsdp", "sp"), None),
    )
    out_specs = (
        P(("fsdp", "sp"), None),
        P(("fsdp", "sp"), None),
        P(("fsdp", "sp"), None),
        P(("fsdp", "sp"), None),
        P("fsdp", None),
        P("fsdp", None),
    )
    return jax.shard_map(shards, mesh=mesh, in_specs=in_specs, out_specs=out_specs, check_vma=False)
```

profile of v0, /device:TPU:1, one launch (start us, length us, event | category | flops | bytes accessed | tf_op | source)
XLA Modules:
  0.0 750.2 jit_solution(3197817629769236512)
XLA Ops:
  10.0 9.7 %all-to-all-start.2 = ((bf16[128,16,128]{0,2,1:T(8,128)(2,1)}), bf16[128,16,128]{0,2,1:T(8,128)(2,1)S(1)}, u32[]{:S(2)}, u32[]{:S(2)}) async-start(bf16[128,16,128]{0,2,1:T(8,128)(2,1)} %bitcast.16), calls=%async_computation.2 | async-start | bytes 1048576 | tf_op jit(solution)/shard_map/all_to_all | solution.py:100
  20.7 12.7 %all-to-all-done.2 = bf16[128,16,128]{0,2,1:T(8,128)(2,1)S(1)} async-done(((bf16[128,16,128]{0,2,1:T(8,128)(2,1)}), bf16[128,16,128]{0,2,1:T(8,128)(2,1)S(1)}, u32[]{:S(2)}, u32[]{:S(2)}) %all-to-all-start.2) | async-done | bytes 524320 | tf_op jit(solution)/shard_map/all_to_all | solution.py:100
  39.4 58.1 %all_gather.10 = bf16[2048,64]{1,0:T(8,128)(2,1)S(1)} all-gather(bf16[64,64]{1,0:T(8,128)(2,1)S(1)} %copy-done.11), channel_id=1, replica_groups=mesh['fsdp'=32,'sp'=16] {'fsdp'}, dimensions={0}, use_global_device_ids=true | all-gather | bytes 270336 | tf_op jit(solution)/shard_map/all_gather | solution.py:95
  98.5 7.7 %all-to-all-start.1 = ((bf16[128,16,128]{2,0,1:T(8,128)(2,1)}), bf16[128,16,128]{2,0,1:T(8,128)(2,1)}, u32[]{:S(2)}, u32[]{:S(2)}) async-start(bf16[128,16,128]{2,0,1:T(8,128)(2,1)} %copy_bitcast_fusion.1), calls=%async_computation.1 | async-start | bytes 1048576 | tf_op jit(solution)/shard_map/all_to_all | solution.py:99
  106.1 42.3 %all_gather.11 = bf16[2048,64]{1,0:T(8,128)(2,1)S(1)} all-gather(bf16[64,64]{1,0:T(8,128)(2,1)S(1)} %copy-done.12), channel_id=1, replica_groups=mesh['fsdp'=32,'sp'=16] {'fsdp'}, dimensions={0}, use_global_device_ids=true | all-gather | bytes 270336 | tf_op jit(solution)/shard_map/all_gather | solution.py:96
  149.8 6.3 fusion.79
  157.4 8.0 %all-to-all-start.4 = ((bf16[128,16,128]{2,0,1:T(8,128)(2,1)}), bf16[128,16,128]{2,0,1:T(8,128)(2,1)}, u32[]{:S(2)}, u32[]{:S(2)}) async-start(bf16[128,16,128]{2,0,1:T(8,128)(2,1)} %bitcast.141), calls=%async_computation.4 | async-start | bytes 1048576 | tf_op jit(solution)/shard_map/all_to_all | solution.py:135
  165.4 28.9 %while.25 = (s32[]{:T(128)}, bf16[4,4,128,1,128]{2,4,1,3,0:T(8,128)(2,1)}, s32[4,4,6]{2,1,0:T(4,128)S(1)}, bf16[16,128,1,128]{3,1,0,2:T(8,128)(2,1)S(1)}, bf16[4...) while((s32[]{:T(128)}, bf16[4,4,128,1,128]{2,4,1,3,0:T(8,128)(2,1)}, ...), condition=%wide.region_3.5_spmd, body=%wide.region_0.4_spmd.sunk | while | flops 204146656 | bytes 11281489 | solution.py:115
  194.3 7.5 %all-to-all-start.3 = ((bf16[16,128,128]{1,2,0:T(8,128)(2,1)}), bf16[16,128,128]{1,2,0:T(8,128)(2,1)}, u32[]{:S(2)}, u32[]{:S(2)}) async-start(bf16[16,128,128]{1,2,0:T(8,128)(2,1)} %bitcast.211), calls=%async_computation.3 | async-start | bytes 1048576 | tf_op jit(solution)/shard_map/all_to_all | solution.py:120
  201.8 157.3 %while.26 = (s32[]{:T(128)}, f32[16,16384]{1,0:T(8,128)}, f32[16,16384]{1,0:T(8,128)}, bf16[4,4,128,1,128]{4,2,1,0,3:T(8,128)(2,1)}, s32[4,4,6]{2,1,0:T(4,128)S(...) while((s32[]{:T(128)}, f32[16,16384]{1,0:T(8,128)}, ...), condition=%wide.region_8.10_spmd.clone, body=%wide.region_4.9_spmd.clone.sunk | while | flops 663688448 | bytes 56507772 | solution.py:170
  209.9 6.3 fusion.145
  216.2 7.0 fusion.144
  247.4 6.3 fusion.145
  253.7 7.0 fusion.144
  287.3 6.3 fusion.145
  293.6 7.0 fusion.144
  327.2 6.3 fusion.145
  333.5 7.0 fusion.144
  359.2 7.7 %all-to-all-start.5 = ((bf16[16,128,128]{2,1,0:T(8,128)(2,1)}), bf16[16,128,128]{2,1,0:T(8,128)(2,1)}, u32[]{:S(2)}, u32[]{:S(2)}) async-start(bf16[16,128,128]{2,1,0:T(8,128)(2,1)} %bitcast.210), calls=%async_computation.5 | async-start | bytes 1048576 | tf_op jit(solution)/shard_map/all_to_all | solution.py:177
  371.6 8.4 %all-to-all-done.5 = bf16[16,128,128]{2,1,0:T(8,128)(2,1)} async-done(((bf16[16,128,128]{2,1,0:T(8,128)(2,1)}), bf16[16,128,128]{2,1,0:T(8,128)(2,1)}, u32[]{:S(2)}, u32[]{:S(2)}) %all-to-all-start.5) | async-done | bytes 524320 | tf_op jit(solution)/shard_map/all_to_all | solution.py:177
  389.8 8.8 %all-to-all-done.7 = bf16[16,128,128]{2,1,0:T(8,128)(2,1)S(1)} async-done(((bf16[16,128,128]{2,1,0:T(8,128)(2,1)}), bf16[16,128,128]{2,1,0:T(8,128)(2,1)S(1)}, u32[]{:S(2)}, u32[]{:S(2)}) %all-to-all-start.7) | async-done | bytes 524320 | tf_op jit(solution)/shard_map/all_to_all | solution.py:179
  398.7 6.3 all-to-all-start.6
  406.9 273.8 %all-reduce.6.cloned.1.call-done = (f32[131072]{0:T(1024)}, f32[131072]{0:T(1024)}) async-done(((f32[131072]{0:T(1024)}, f32[131072]{0:T(1024)}), (f32[131072]{0:T(1024)}, f32[131072]{0:T(1024)})) %all-reduce.6.cloned.1.call-update) | async-done | bytes 1048592
  682.1 48.9 %all-reduce.3 = (f32[4096]{0:T(1024)S(1)}, f32[4096]{0:T(1024)S(1)}) all-reduce(f32[4096]{0:T(1024)S(1)} %dynamic-slice.1, f32[4096]{0:T(1024)S(1)} %dynamic-slice.3), channel_id=1, replica_groups=mesh['fsdp'=32,'sp'=16] {'sp'}, use_global_device_ids=true, to_apply=%region_9.11 | all-reduce | flops 8192 | bytes 65536 | tf_op jit(solution)/shard_map/psum | solution.py:150
  (204 shorter events, 175.5 us)
Async XLA Ops:
  7.2 141.4 %copy-start = (bf16[128,2048]{1,0:T(8,128)(2,1)S(1)}, bf16[128,2048]{1,0:T(8,128)(2,1)}, u32[]{:S(2)}) copy-start(bf16[128,2048]{1,0:T(8,128)(2,1)} %param.21) | copy-start | bytes 1572868
  7.2 12.5 %copy-start.9 = (bf16[128,2048]{1,0:T(8,128)(2,1)S(1)}, bf16[128,2048]{1,0:T(8,128)(2,1)}, u32[]{:S(2)}) copy-start(bf16[128,2048]{1,0:T(8,128)(2,1)} %param.16) | copy-start | bytes 1572868
  7.2 142.6 %all-gather.2.cloned.1.call-start = ((), (), s32[]{:S(2)}) async-start(), calls=%async_computation.8 | async-start | bytes 8650752 | tf_op jit(solution)/shard_map/all_gather | solution.py:94
  10.0 29.4 %copy-start.11 = (bf16[64,64]{1,0:T(8,128)(2,1)S(1)}, bf16[64,64]{1,0:T(8,128)(2,1)}, u32[]{:S(2)}) copy-start(bf16[64,64]{1,0:T(8,128)(2,1)} %param.19) | copy-start | bytes 24580
  10.0 23.4 %all-to-all-start.2 = ((bf16[128,16,128]{0,2,1:T(8,128)(2,1)}), bf16[128,16,128]{0,2,1:T(8,128)(2,1)S(1)}, u32[]{:S(2)}, u32[]{:S(2)}) async-start(bf16[128,16,128]{0,2,1:T(8,128)(2,1)} %bitcast.16), calls=%async_computation.2 | async-start | bytes 1048576 | tf_op jit(solution)/shard_map/all_to_all | solution.py:100
  19.7 77.8 %copy-start.10 = (bf16[128,2048]{1,0:T(8,128)(2,1)S(1)}, bf16[128,2048]{1,0:T(8,128)(2,1)}, u32[]{:S(2)}) copy-start(bf16[128,2048]{1,0:T(8,128)(2,1)} %param.14) | copy-start | bytes 1572868
  33.4 65.0 %all-to-all-start = ((bf16[128,16,128]{0,2,1:T(8,128)(2,1)}), bf16[128,16,128]{0,2,1:T(8,128)(2,1)S(1)}, u32[]{:S(2)}, u32[]{:S(2)}) async-start(bf16[128,16,128]{0,2,1:T(8,128)(2,1)} %bitcast.11), calls=%async_computation | async-start | bytes 1048576 | tf_op jit(solution)/shard_map/all_to_all | solution.py:101
  39.4 66.7 %copy-start.12 = (bf16[64,64]{1,0:T(8,128)(2,1)S(1)}, bf16[64,64]{1,0:T(8,128)(2,1)}, u32[]{:S(2)}) copy-start(bf16[64,64]{1,0:T(8,128)(2,1)} %param.20) | copy-start | bytes 24580
  39.4 109.1 %copy-start.13 = (s32[1,16,6]{1,0,2:T(1,128)S(1)}, s32[1,16,6]{1,0,2:T(1,128)}, u32[]{:S(2)}) copy-start(s32[1,16,6]{1,0,2:T(1,128)} %param.17) | copy-start | bytes 1156
  97.5 58.6 %copy-start.7 = (bf16[2048,64]{1,0:T(8,128)(2,1)}, bf16[2048,64]{1,0:T(8,128)(2,1)S(1)}, u32[]{:S(2)}) copy-start(bf16[2048,64]{1,0:T(8,128)(2,1)S(1)} %all_gather.10) | copy-start | bytes 786436
  98.5 59.0 %all-to-all-start.1 = ((bf16[128,16,128]{2,0,1:T(8,128)(2,1)}), bf16[128,16,128]{2,0,1:T(8,128)(2,1)}, u32[]{:S(2)}, u32[]{:S(2)}) async-start(bf16[128,16,128]{2,0,1:T(8,128)(2,1)} %copy_bitcast_fusion.1), calls=%async_computation.1 | async-start | bytes 1048576 | tf_op jit(solution)/shard_map/all_to_all | solution.py:99
  157.4 36.9 %all-to-all-start.4 = ((bf16[128,16,128]{2,0,1:T(8,128)(2,1)}), bf16[128,16,128]{2,0,1:T(8,128)(2,1)}, u32[]{:S(2)}, u32[]{:S(2)}) async-start(bf16[128,16,128]{2,0,1:T(8,128)(2,1)} %bitcast.141), calls=%async_computation.4 | async-start | bytes 1048576 | tf_op jit(solution)/shard_map/all_to_all | solution.py:135
  194.3 164.9 %all-to-all-start.3 = ((bf16[16,128,128]{1,2,0:T(8,128)(2,1)}), bf16[16,128,128]{1,2,0:T(8,128)(2,1)}, u32[]{:S(2)}, u32[]{:S(2)}) async-start(bf16[16,128,128]{1,2,0:T(8,128)(2,1)} %bitcast.211), calls=%async_computation.3 | async-start | bytes 1048576 | tf_op jit(solution)/shard_map/all_to_all | solution.py:120
  216.2 7.0 copy-start.2
  253.7 7.0 copy-start.2
  293.6 7.0 copy-start.2
  333.5 7.0 copy-start.2
  359.2 10.6 %copy-start.3 = (f32[16,16384]{1,0:T(8,128)S(1)}, f32[16,16384]{1,0:T(8,128)}, u32[]{:S(2)}) copy-start(f32[16,16384]{1,0:T(8,128)} %get-tuple-element.91) | copy-start | bytes 3145732
  359.2 10.6 %copy-start.4 = (f32[16,16384]{1,0:T(8,128)S(1)}, f32[16,16384]{1,0:T(8,128)}, u32[]{:S(2)}) copy-start(f32[16,16384]{1,0:T(8,128)} %get-tuple-element.90) | copy-start | bytes 3145732
  359.2 20.8 %all-to-all-start.5 = ((bf16[16,128,128]{2,1,0:T(8,128)(2,1)}), bf16[16,128,128]{2,1,0:T(8,128)(2,1)}, u32[]{:S(2)}, u32[]{:S(2)}) async-start(bf16[16,128,128]{2,1,0:T(8,128)(2,1)} %bitcast.210), calls=%async_computation.5 | async-start | bytes 1048576 | tf_op jit(solution)/shard_map/all_to_all | solution.py:177
  379.9 18.8 %all-to-all-start.7 = ((bf16[16,128,128]{2,1,0:T(8,128)(2,1)}), bf16[16,128,128]{2,1,0:T(8,128)(2,1)S(1)}, u32[]{:S(2)}, u32[]{:S(2)}) async-start(bf16[16,128,128]{2,1,0:T(8,128)(2,1)} %bitcast.73), calls=%async_computation.7 | async-start | bytes 1048576 | tf_op jit(solution)/shard_map/all_to_all | solution.py:179
  385.9 294.8 %all-reduce.6.cloned.1.call-start = ((), (), s32[]{:S(2)}) async-start(), calls=%async_computation.9 | async-start | bytes 2097152
  398.7 343.3 %all-to-all-start.6 = ((bf16[16,128,128]{2,1,0:T(8,128)(2,1)}), bf16[16,128,128]{2,1,0:T(8,128)(2,1)S(1)}, u32[]{:S(2)}, u32[]{:S(2)}) async-start(bf16[16,128,128]{2,1,0:T(8,128)(2,1)} %bitcast.71), calls=%async_computation.6 | async-start | bytes 1048576 | tf_op jit(solution)/shard_map/all_to_all | solution.py:178
  732.4 4.9 copy-start.6
  (6 other events, 11.8 us)
Sparse Core Ops, SparseCore 0:
  11.2 102.0 all-gather.1
  389.7 290.9 all-reduce.5
where the time goes:
time: 764 us; the launch traced here: 750 us
  waiting for transfers between devices  304 us (40%)
  blocking collectives  149 us (20%)
  matrix products  139 us (18%)
  local copies, waits for them, and re-layouts  71.6 us (9%)
  starting transfers between devices  58.8 us (8%)
  between operations  15 us (2%)
  other arithmetic  11.5 us (2%)
    unnamed x3, waiting for transfers between devices  274 us
    all_gather x1, blocking collectives, shards(): lax.all_gather(adapter_down_weight, 'fsdp', axis=0, tiled=True)  58.1 us
    psum x1, blocking collectives, shards(): summed_down, summed_up = lax.psum((partial_down, partial_up), 'sp')  48.9 us
    all_gather x1, blocking collectives, shards(): lax.all_gather(adapter_up_weight_transposed, 'fsdp', axis=0, tiled=True)  42.3 us
    dot_general x4, matrix products, backward_group(): jnp.einsum('ghqk,gqhd->gkhd', dscores, query_group, preferred_element_typ...  28 us
    dot_general x4, matrix products, backward_group(): jnp.einsum('ghqk,gkhd->gqhd', dscores, keys_gathered, preferred_element_t...  25.2 us
    sub x8, matrix products, block_probs(): raised = jnp.exp(scores - highest)  19.2 us
  transfers between devices with their start and end apart: 10, of which 4 were waited for; matrix products, arithmetic and copies ran while one was open for 29% of the time, Pallas kernels for 0%

commit v1 on v0

v1 whole, which is shorter than its diff:
```python
import math

import jax
import jax.numpy as jnp
from jax import lax
from jax.experimental import pallas as pl
from jax.experimental.pallas import tpu as pltpu
from jax.sharding import PartitionSpec as P

MODEL_WIDTH = 2048
HEADS = 16
BLOCK = 128
KEY_BLOCKS = 6
ADAPTER_RANK = 64
TOKENS = 65536

NZ, NX = 4, 4
NL, NY = 2, 8
NB = NL * NY
SHARD = 64
RANDOM = 2 * NB

MESH = pl.DeviceIdType.MESH
F32 = jnp.float32
BF16 = jnp.bfloat16


def dot(a, b, ca, cb):
    return lax.dot_general(a, b, (((ca,), (cb,)), ((), ())), preferred_element_type=F32)


def drain(ref, sem):
    pltpu.make_async_copy(ref, ref, sem).wait()


def kernel(
    q_ref,
    k_ref,
    v_ref,
    blk,
    w_ref,
    a_ref,
    b_ref,
    cot,
    mixed_ref,
    dq_ref,
    dk_ref,
    dv_ref,
    gd_ref,
    gu_ref,
    qh,
    kh,
    vh,
    gh,
    ctx_heads,
    dctx_send,
    ctx,
    dqb,
    dkb,
    dvb,
    wfull,
    ab,
    probs,
    wts,
    dsc,
    pre_k,
    pre_v,
    d0,
    part,
    rc,
    s1,
    rx,
    s2,
    rz,
    s3,
    rl,
    s4,
    ry,
    s5,
    gfin,
    rank,
    perm,
    same,
    last,
    has,
    qkv_s,
    qkv_r,
    blk_s,
    blk_r,
    abz_s,
    abz_r,
    wz_s,
    wz_r,
    wx_s,
    wx_r,
    wc_s,
    wc_r,
    own_sem,
    red_s,
    red_r,
):
    f = lax.axis_index("fsdp")
    j = lax.axis_index("sp")
    z, x, c = f // (2 * NX), (f // 2) % NX, f % 2
    zl, y = j // NY, j % NY
    oc = 1 - c
    scaling = 1.0 / math.sqrt(BLOCK)
    log2e = 1.4426950408889634

    def fid(zz, xx, cc):
        return zz * (2 * NX) + xx * 2 + cc

    def sp_peer(d):
        return (j + d) % NB

    sibling = (fid(z, x, oc), j)

    def xpeer(d):
        return (fid(z, (x + d) % NX, c), j)

    def zpeer(d):
        return (fid((z + d) % NZ, x, c), j)

    def remote(src, dst, ssem, rsem, dev):
        pltpu.make_async_remote_copy(
            src_ref=src, dst_ref=dst, send_sem=ssem, recv_sem=rsem, device_id=dev, device_id_type=MESH
        ).start()

    def cols(h):
        return pl.ds(pl.multiple_of(h * BLOCK, BLOCK), BLOCK)

    barrier = pltpu.get_barrier_semaphore()

    def greet(d, carry):
        pl.semaphore_signal(barrier, inc=1, device_id=(f, sp_peer(d)), device_id_type=MESH)
        return carry

    lax.fori_loop(1, NB, greet, 0)
    for d in (1, 2, 3):
        pl.semaphore_signal(barrier, inc=1, device_id=xpeer(d), device_id_type=MESH)
        pl.semaphore_signal(barrier, inc=1, device_id=zpeer(d), device_id_type=MESH)
    pl.semaphore_signal(barrier, inc=1, device_id=sibling, device_id_type=MESH)
    pl.semaphore_wait(barrier, NB - 1 + 7)

    ab[z, x, c] = jnp.concatenate([a_ref[...], b_ref[...]], axis=1)
    for d in (1, 3, 2):
        remote(ab.at[z, x, c], ab.at[z, x, c], abz_s.at[0], abz_r.at[0], zpeer(d))

    for n, (src, dst) in enumerate(((k_ref, kh), (q_ref, qh), (v_ref, vh))):

        def send_heads(d, carry, src=src, dst=dst, n=n):
            h = sp_peer(d)
            remote(src.at[:, cols(h)], dst.at[j], qkv_s.at[n], qkv_r.at[n], (f, h))
            return carry

        lax.fori_loop(1, NB, send_heads, 0)
        pltpu.make_async_copy(src.at[:, cols(j)], dst.at[j], qkv_r.at[n]).start()
        if n == 0:
            for d in (1, 3, 2):
                remote(w_ref, wfull.at[z, x, c], wz_s, wz_r.at[z], zpeer(d))
            pltpu.make_async_copy(w_ref, wfull.at[z, x, c], own_sem).start()
            remote(w_ref, wfull.at[z, x, c], wc_s, wc_r.at[z, x], sibling)
            drain(ab.at[0, pl.ds(0, 3), 0], abz_r.at[0])
            for d in (1, 3, 2):
                remote(ab.at[:, x, c], ab.at[:, x, c], abz_s.at[1], abz_r.at[1], xpeer(d))
            for d in (1, 3, 2):
                remote(w_ref, wfull.at[z, x, c], wx_s, wx_r.at[z, x], xpeer(d))

    def entry(r):
        return blk[0, r // 2, 4 + r % 2]

    def rank_of(r, carry):
        mine = entry(r) * RANDOM + r
        total = jnp.int32(0)
        for s in range(RANDOM):
            total = total + jnp.where(entry(s) * RANDOM + s < mine, 1, 0)
        rank[r] = total
        return carry

    lax.fori_loop(0, RANDOM, rank_of, 0)

    def perm_of(p, carry):
        total = jnp.int32(0)
        for s in range(RANDOM):
            total = total + jnp.where(rank[s] == p, s, 0)
        perm[p] = total
        named = blk[0, total // 2, 4 + total % 2]
        same[p] = jnp.where(named == carry, 1.0, 0.0).astype(F32)
        return named

    lax.fori_loop(0, RANDOM, perm_of, jnp.int32(-1))

    def last_of(n, carry):
        upto = jnp.int32(0)
        equal = jnp.int32(0)
        for s in range(RANDOM):
            upto = upto + jnp.where(entry(s) <= n, 1, 0)
            equal = equal + jnp.where(entry(s) == n, 1, 0)
        last[n] = jnp.maximum(upto - 1, 0)
        has[n] = jnp.where(equal > 0, 1.0, 0.0).astype(F32)
        return carry

    lax.fori_loop(0, NB, last_of, 0)

    drain(ab.at[pl.ds(0, 3), :, 0], abz_r.at[1])
    remote(ab.at[:, :, c], ab.at[:, :, c], abz_s.at[2], abz_r.at[2], sibling)

    def forward_z(d):
        u = (z + d) % NZ
        piece = wfull.at[u, x, c]
        drain(piece, wz_r.at[u])
        for e in (1, 3, 2):
            remote(piece, piece, wx_s, wx_r.at[u, x], xpeer(e))
        remote(piece, piece, wc_s, wc_r.at[u, x], sibling)

    def forward_x(d):
        u = (z + d) % NZ
        for e in (1, 3, 2):
            xx = (x + e) % NX
            piece = wfull.at[u, xx, c]
            drain(piece, wx_r.at[u, xx])
            remote(piece, piece, wc_s, wc_r.at[u, xx], sibling)

    def context_gradient(d):
        u = (z + d) % NZ

        def one_head(e, carry):
            xx = (x + e) % NX
            h = u * NX + xx
            drain(wfull.at[u, xx, oc], wc_r.at[u, xx])
            rows = wfull[u, xx].reshape(BLOCK, MODEL_WIDTH)
            adapter = ab[u, xx].reshape(BLOCK, 2 * ADAPTER_RANK)
            g = dot(cot[...], rows, 1, 1) + dot(d0[...], adapter, 1, 1)
            dctx_send[h] = g.astype(BF16)

            @pl.when(h != j)
            def _():
                remote(dctx_send.at[h], gh.at[j], blk_s.at[1], blk_r.at[1], (f, h))

            @pl.when(h == j)
            def _():
                pltpu.make_async_copy(dctx_send.at[h], gh.at[j], blk_r.at[1]).start()

            return carry

        lax.fori_loop(0, NX, one_head, 0)

    forward_z(1)
    forward_z(3)
    forward_x(0)

    drain(w_ref, own_sem)
    drain(ab.at[:, :, 0], abz_r.at[2])
    lane = lax.broadcasted_iota(jnp.int32, (BLOCK, 2 * ADAPTER_RANK), 1)
    both = dot(cot[...], ab[...].reshape(MODEL_WIDTH, 2 * ADAPTER_RANK), 1, 0)
    d0[...] = jnp.where(lane < ADAPTER_RANK, pltpu.roll(both, ADAPTER_RANK, 1), 0.0).astype(BF16)

    context_gradient(0)
    forward_z(2)
    forward_x(1)
    forward_x(3)
    context_gradient(1)

    drain(kh, qkv_r.at[0])
    drain(qh, qkv_r.at[1])
    drain(vh, qkv_r.at[2])

    def gathered(ref, i):
        return jnp.concatenate([ref[blk[0, i, s]] for s in range(KEY_BLOCKS)], axis=0)

    def send_block(src, dst_ref, n, i):
        @pl.when(i != j)
        def _():
            remote(src.at[i], dst_ref.at[:, cols(j)], blk_s.at[n], blk_r.at[n], (f, i))

        @pl.when(i == j)
        def _():
            pltpu.make_async_copy(src.at[i], dst_ref.at[:, cols(j)], blk_r.at[n]).start()

    def forward_block(t, carry):
        i = sp_peer(t)
        scores = dot(gathered(kh, i), qh[i], 1, 1)
        highest = jnp.max(scores, axis=0, keepdims=True)
        raised = jnp.exp2((scores - highest) * (scaling * log2e))
        p = raised * (1.0 / jnp.sum(raised, axis=0, keepdims=True))
        probs[i] = p
        w = p.astype(BF16)
        wts[i] = w.reshape(KEY_BLOCKS, BLOCK, BLOCK)
        ctx_heads[i] = dot(w, gathered(vh, i), 0, 0).astype(BF16)
        send_block(ctx_heads, ctx, 0, i)
        return carry

    lax.fori_loop(1, NB + 1, forward_block, 0)

    context_gradient(3)
    forward_x(2)
    context_gradient(2)
    drain(gh, blk_r.at[1])

    def backward_block(t, carry):
        i = sp_peer(t)
        p = probs[i]
        dw = dot(gathered(vh, i), gh[i], 1, 1)
        correction = jnp.sum(p * dw, axis=0, keepdims=True)
        ds = (p * (dw - correction) * scaling).astype(BF16)
        dsc[i] = ds.reshape(KEY_BLOCKS, BLOCK, BLOCK)
        dqb[i] = dot(ds, gathered(kh, i), 0, 0).astype(BF16)
        send_block(dqb, dq_ref, 2, i)
        return carry

    lax.fori_loop(1, NB + 1, backward_block, 0)

    def random_terms(p, carry):
        r = perm[p]
        i = r // 2
        slot = 4 + r % 2
        keep = same[p]
        acc_k = carry[0] * keep + dot(dsc[i, slot], qh[i], 1, 0)
        acc_v = carry[1] * keep + dot(wts[i, slot], gh[i], 1, 0)
        pre_k[p] = acc_k
        pre_v[p] = acc_v
        return acc_k, acc_v

    zero = jnp.zeros((BLOCK, BLOCK), F32)
    lax.fori_loop(0, RANDOM, random_terms, (zero, zero))

    def common_terms(i, carry):
        return (
            carry[0] + dot(dsc[i, 3], qh[i], 1, 0),
            carry[1] + dot(wts[i, 3], gh[i], 1, 0),
        )

    common_k, common_v = lax.fori_loop(0, NB, common_terms, (zero, zero))
    pre_k[RANDOM] = common_k
    pre_v[RANDOM] = common_v
    common = blk[0, 0, 3]

    def key_block(t, carry):
        n = sp_peer(t)
        before, after = (n + NB - 1) % NB, (n + 1) % NB
        slot_before = jnp.where(blk[0, before, 2] == n, 2, 0)
        slot_after = jnp.where(blk[0, after, 0] == n, 0, 2)
        is_common = jnp.where(common == n, 1.0, 0.0).astype(F32)

        def total(terms, rows, pre):
            window = (
                dot(terms[n, 1], rows[n], 1, 0)
                + dot(terms[before, slot_before], rows[before], 1, 0)
                + dot(terms[after, slot_after], rows[after], 1, 0)
            )
            return (window + pre[last[n]] * has[n] + pre[RANDOM] * is_common).astype(BF16)

        dkb[n] = total(dsc, qh, pre_k)
        send_block(dkb, dk_ref, 3, n)
        dvb[n] = total(wts, gh, pre_v)
        send_block(dvb, dv_ref, 4, n)
        return carry

    lax.fori_loop(1, NB + 1, key_block, 0)

    drain(ctx, blk_r.at[0])
    both = dot(ctx[...], ab[...].reshape(MODEL_WIDTH, 2 * ADAPTER_RANK), 1, 0)
    low = jnp.where(lane >= ADAPTER_RANK, pltpu.roll(both, ADAPTER_RANK, 1), 0.0).astype(BF16)
    normal = 1.0 / math.sqrt(TOKENS)

    def partial(h, carry):
        s = dot(ctx[:, cols(h)], d0[...], 0, 0) + dot(cot[:, cols(h)], low, 0, 0)
        part[h // NX, h % NX] = (s * normal).reshape(2, SHARD, BLOCK)
        return carry

    lax.fori_loop(0, HEADS, partial, 0)
    remote(part.at[:, :, oc], rc, red_s.at[0], red_r.at[0], sibling)

    wide = 256

    def output_columns(n, carry):
        rows = wfull[:, :, :, :, pl.ds(pl.multiple_of(n * wide, wide), wide)]
        adapter = ab[n // 2, pl.ds(2 * (n % 2), 2)].reshape(wide, 2 * ADAPTER_RANK)
        m = dot(ctx[...], rows.reshape(MODEL_WIDTH, wide), 1, 0) + dot(low, adapter, 1, 1)
        mixed_ref[:, pl.ds(pl.multiple_of(n * wide, wide), wide)] = m.astype(BF16)
        return carry

    lax.fori_loop(0, MODEL_WIDTH // wide, output_columns, 0)

    drain(rc, red_r.at[0])

    def add_core(u, carry):
        s1[u] = part[u, :, c] + rc[u]
        return carry

    lax.fori_loop(0, NZ, add_core, 0)
    for e in (1, 3, 2):
        remote(s1.at[:, (x + e) % NX], rx.at[x], red_s.at[1], red_r.at[1], xpeer(e))
    drain(rx.at[pl.ds(0, 3)], red_r.at[1])
    s2[...] = s1[:, x] + rx[(x + 1) % NX] + rx[(x + 2) % NX] + rx[(x + 3) % NX]
    for e in (1, 3, 2):
        remote(s2.at[(z + e) % NZ], rz.at[z], red_s.at[2], red_r.at[2], zpeer(e))
    drain(rz.at[pl.ds(0, 3)], red_r.at[2])
    s3[...] = s2[z] + rz[(z + 1) % NZ] + rz[(z + 2) % NZ] + rz[(z + 3) % NZ]
    remote(s3, rl, red_s.at[3], red_r.at[3], (f, (1 - zl) * NY + y))
    drain(rl, red_r.at[3])
    s4[...] = (s3[...] + rl[...]).reshape(NY, 8, BLOCK)
    for e in range(1, NY):
        yy = (y + e) % NY
        remote(s4.at[yy], ry.at[y], red_s.at[4], red_r.at[4], (f, zl * NY + yy))
    drain(ry.at[pl.ds(0, NY - 1)], red_r.at[4])
    total = s4[y]
    for e in range(1, NY):
        total = total + ry[(y + e) % NY]
    s5[...] = total
    gfin[y] = total
    for e in range(1, NY):
        yy = (y + e) % NY
        remote(s5, gfin.at[y], red_s.at[5], red_r.at[5], (f, zl * NY + yy))
    drain(ry.at[pl.ds(0, NY - 1)], red_r.at[5])
    both = gfin[...].reshape(SHARD, BLOCK)
    gd_ref[...] = both[:, :ADAPTER_RANK]
    gu_ref[...] = both[:, ADAPTER_RANK:]

    drain(dq_ref, blk_r.at[2])
    drain(dk_ref, blk_r.at[3])
    drain(dv_ref, blk_r.at[4])
    for n in range(3):
        drain(qh.at[pl.ds(0, NB - 1)], qkv_s.at[n])
    for n in range(5):
        drain(qh.at[pl.ds(0, NB - 1)], blk_s.at[n])
    drain(ab.at[0, pl.ds(0, 3), 0], abz_s.at[0])
    drain(ab.at[pl.ds(0, 3), :, 0], abz_s.at[1])
    drain(ab.at[:, :, 0], abz_s.at[2])
    drain(wfull.at[0, pl.ds(0, 3), 0], wz_s)
    drain(wfull.at[pl.ds(0, 3), :, 0], wx_s)
    drain(wfull.at[:, :, 0], wc_s)
    drain(rc, red_s.at[0])
    drain(rx.at[pl.ds(0, 3)], red_s.at[1])
    drain(rz.at[pl.ds(0, 3)], red_s.at[2])
    drain(rl, red_s.at[3])
    drain(ry.at[pl.ds(0, NY - 1)], red_s.at[4])
    drain(ry.at[pl.ds(0, NY - 1)], red_s.at[5])


def shards(q, k, v, blocks, w, a, b, cot):
    hbm = pl.BlockSpec(memory_space=pl.ANY)
    vmem = pl.BlockSpec(memory_space=pltpu.VMEM)
    smem = pl.BlockSpec(memory_space=pltpu.SMEM)
    dma = pltpu.SemaphoreType.DMA
    blocks3 = pltpu.VMEM((NB, BLOCK, BLOCK), BF16)
    tokens = jax.ShapeDtypeStruct((BLOCK, MODEL_WIDTH), BF16)
    grad = jax.ShapeDtypeStruct((SHARD, ADAPTER_RANK), F32)
    return pl.pallas_call(
        kernel,
        out_shape=(tokens, tokens, tokens, tokens, grad, grad),
        in_specs=[hbm, hbm, hbm, smem, hbm, vmem, vmem, vmem],
        out_specs=(vmem, hbm, hbm, hbm, vmem, vmem),
        scratch_shapes=[
            blocks3,
            blocks3,
            blocks3,
            blocks3,
            blocks3,
            blocks3,
            pltpu.VMEM((BLOCK, MODEL_WIDTH), BF16),
            blocks3,
            blocks3,
            blocks3,
            pltpu.VMEM((NZ, NX, 2, SHARD, MODEL_WIDTH), BF16),
            pltpu.VMEM((NZ, NX, 2, SHARD, 2 * ADAPTER_RANK), BF16),
            pltpu.VMEM((NB, KEY_BLOCKS * BLOCK, BLOCK), F32),
            pltpu.VMEM((NB, KEY_BLOCKS, BLOCK, BLOCK), BF16),
            pltpu.VMEM((NB, KEY_BLOCKS, BLOCK, BLOCK), BF16),
            pltpu.VMEM((RANDOM + 1, BLOCK, BLOCK), F32),
            pltpu.VMEM((RANDOM + 1, BLOCK, BLOCK), F32),
            pltpu.VMEM((BLOCK, 2 * ADAPTER_RANK), BF16),
            pltpu.VMEM((NZ, NX, 2, SHARD, BLOCK), F32),
            pltpu.VMEM((NZ, NX, SHARD, BLOCK), F32),
            pltpu.VMEM((NZ, NX, SHARD, BLOCK), F32),
            pltpu.VMEM((NX, NZ, SHARD, BLOCK), F32),
            pltpu.VMEM((NZ, SHARD, BLOCK), F32),
            pltpu.VMEM((NZ, SHARD, BLOCK), F32),
            pltpu.VMEM((SHARD, BLOCK), F32),
            pltpu.VMEM((SHARD, BLOCK), F32),
            pltpu.VMEM((NY, 8, BLOCK), F32),
            pltpu.VMEM((NY, 8, BLOCK), F32),
            pltpu.VMEM((8, BLOCK), F32),
            pltpu.VMEM((NY, 8, BLOCK), F32),
            pltpu.SMEM((RANDOM,), jnp.int32),
            pltpu.SMEM((RANDOM,), jnp.int32),
            pltpu.SMEM((RANDOM,), F32),
            pltpu.SMEM((NB,), jnp.int32),
            pltpu.SMEM((NB,), F32),
            dma((3,)),
            dma((3,)),
            dma((5,)),
            dma((5,)),
            dma((3,)),
            dma((3,)),
            dma,
            dma((NZ,)),
            dma,
            dma((NZ, NX)),
            dma,
            dma((NZ, NX)),
            dma,
            dma((6,)),
            dma((6,)),
        ],
        compiler_params=pltpu.CompilerParams(
            collective_id=0, has_side_effects=True, vmem_limit_bytes=60 * 2**20
        ),
    )(q, k, v, blocks, w, a, b, cot)


def solution(mesh):
    rows = P(("fsdp", "sp"), None)
    return jax.shard_map(
        shards,
        mesh=mesh,
        in_specs=(rows, rows, rows, P("fsdp", None, None), P("fsdp", None), P("fsdp", None), P("fsdp", None), rows),
        out_specs=(rows, rows, rows, rows, P("fsdp", None), P("fsdp", None)),
        check_vma=False,
    )
```

time: 764 us -> 161 us (0.21)
  the two profiles are of different devices: /device:TPU:1 before, /device:TPU:6 now
where the time goes in v1:
time: 161 us
  Pallas kernels  152 us (94%)
  local copies, waits for them, and re-layouts  7.94 us (5%)
    pallas_call x1, Pallas kernels, shards(): pl.pallas_call(kernel, out_shape=(tokens, tokens, tokens, tokens, grad, g...  152 us
    unnamed x17, local copies, waits for them, and re-layouts  7.94 us

profile of v1, /device:TPU:6, one launch (start us, length us, event | category | flops | bytes accessed | tf_op | source)
XLA Modules:
  0.0 160.8 jit_solution(12974924701447211672)
XLA Ops:
  0.6 1.4 copy.14.blk
  2.0 152.2 %shard_map.127 = (bf16[128,2048]{1,0:T(8,128)(2,1)}, bf16[128,2048]{1,0:T(8,128)(2,1)}, bf16[128,2048]{1,0:T(8,128)(2,1)}, bf16[128,2048]{1,0:T(8,128)(2,1)}, f32[64,64]{1,0:T(8,128)}, /*index=5*/f32[64,64]{1,0:T(8,128)}) custom-call(bf16[128,2048]{1,0:T(8,128)(2,1)} %q_ref.1, bf16[128,2048]{1,0:T(8,128)(2,1)} %k_ref.1, bf16[128,2048]{1,0:T(8,128)(2,1)} %v_ref.1, ...), custom_call_target="tpu_custom_call" | custom-call | tf_op jit(solution)/shard_map/pallas_call | solution.py:449
  154.2 0.0 copy-start.2
  154.2 1.9 %copy.21 = bf16[128,2048]{1,0:T(8,128)(2,1)} copy(bf16[128,2048]{1,0:T(8,128)(2,1)} %get-tuple-element.12) | data formatting | bytes 1048576
  156.2 0.0 copy-done.2
  156.2 0.0 copy-start.1
  156.2 0.8 copy.22
  157.0 0.4 copy-done.1
  157.4 0.0 copy-start
  157.4 0.8 copy.23
  158.2 0.4 copy-done
  158.6 0.0 copy-start.4
  158.6 0.8 copy.24
  159.4 0.0 copy-done.4
  159.4 0.0 copy-start.3
  159.4 0.6 copy.25
  160.1 0.2 copy-done.3
  160.2 0.6 copy.26
Async XLA Ops:
  154.2 2.0 %copy-start.2 = (bf16[128,2048]{1,0:T(8,128)(2,1)S(1)}, bf16[128,2048]{1,0:T(8,128)(2,1)}, u32[]{:S(2)}) copy-start(bf16[128,2048]{1,0:T(8,128)(2,1)} %get-tuple-element.13) | copy-start | bytes 1572868
  156.2 1.2 copy-start.1
  157.4 1.2 copy-start
  158.6 0.8 copy-start.4
  159.4 0.8 copy-start.3

commit v2 on v1

--- a/solution.py
+++ b/solution.py
@@ -66,6 +66,7 @@
     pre_k,
     pre_v,
     d0,
+    l0,
     part,
     rc,
     s1,
@@ -121,6 +122,10 @@
     def zpeer(d):
         return (fid((z + d) % NZ, x, c), j)
 
+    side = 1 - 2 * zl
+    pair = (f, (1 - zl) * NY + y)
+    outer = (fid((z - side + NZ) % NZ, x, c), (1 - zl) * NY + y)
+
     def remote(src, dst, ssem, rsem, dev):
         pltpu.make_async_remote_copy(
             src_ref=src, dst_ref=dst, send_sem=ssem, recv_sem=rsem, device_id=dev, device_id_type=MESH
@@ -140,7 +145,8 @@
         pl.semaphore_signal(barrier, inc=1, device_id=xpeer(d), device_id_type=MESH)
         pl.semaphore_signal(barrier, inc=1, device_id=zpeer(d), device_id_type=MESH)
     pl.semaphore_signal(barrier, inc=1, device_id=sibling, device_id_type=MESH)
-    pl.semaphore_wait(barrier, NB - 1 + 7)
+    pl.semaphore_signal(barrier, inc=1, device_id=outer, device_id_type=MESH)
+    pl.semaphore_wait(barrier, NB - 1 + 8)
 
     ab[z, x, c] = jnp.concatenate([a_ref[...], b_ref[...]], axis=1)
     for d in (1, 3, 2):
@@ -156,18 +162,17 @@
         lax.fori_loop(1, NB, send_heads, 0)
         pltpu.make_async_copy(src.at[:, cols(j)], dst.at[j], qkv_r.at[n]).start()
         if n == 0:
-            for d in (1, 3, 2):
-                remote(w_ref, wfull.at[z, x, c], wz_s, wz_r.at[z], zpeer(d))
+            remote(w_ref, wfull.at[z, x, c], wz_s, wz_r.at[z], outer)
             pltpu.make_async_copy(w_ref, wfull.at[z, x, c], own_sem).start()
             remote(w_ref, wfull.at[z, x, c], wc_s, wc_r.at[z, x], sibling)
             drain(ab.at[0, pl.ds(0, 3), 0], abz_r.at[0])
             for d in (1, 3, 2):
                 remote(ab.at[:, x, c], ab.at[:, x, c], abz_s.at[1], abz_r.at[1], xpeer(d))
-            for d in (1, 3, 2):
+            for d in (1, 3):
                 remote(w_ref, wfull.at[z, x, c], wx_s, wx_r.at[z, x], xpeer(d))
 
     def entry(r):
-        return blk[0, r // 2, 4 + r % 2]
+        return blk[4 + r % 2, 0, r // 2]
 
     def rank_of(r, carry):
         mine = entry(r) * RANDOM + r
@@ -184,7 +189,7 @@
         for s in range(RANDOM):
             total = total + jnp.where(rank[s] == p, s, 0)
         perm[p] = total
-        named = blk[0, total // 2, 4 + total % 2]
+        named = blk[4 + total % 2, 0, total // 2]
         same[p] = jnp.where(named == carry, 1.0, 0.0).astype(F32)
         return named
 
@@ -205,25 +210,34 @@
     drain(ab.at[pl.ds(0, 3), :, 0], abz_r.at[1])
     remote(ab.at[:, :, c], ab.at[:, :, c], abz_s.at[2], abz_r.at[2], sibling)
 
-    def forward_z(d):
-        u = (z + d) % NZ
+    mine, near, next_, far = z, (z - side + NZ) % NZ, (z + side + NZ) % NZ, (z + 2) % NZ
+    left, right = (x + NX - 1) % NX, (x + 1) % NX
+    half = SHARD // 2
+
+    def forward_z(u, onward):
         piece = wfull.at[u, x, c]
         drain(piece, wz_r.at[u])
-        for e in (1, 3, 2):
+        if onward is not None:
+            remote(piece, piece, wz_s, wz_r.at[u], onward)
+        for e in (1, 3):
             remote(piece, piece, wx_s, wx_r.at[u, x], xpeer(e))
         remote(piece, piece, wc_s, wc_r.at[u, x], sibling)
 
-    def forward_x(d):
-        u = (z + d) % NZ
-        for e in (1, 3, 2):
-            xx = (x + e) % NX
+    def forward_x(u):
+        for xx, start, e in ((left, 0, 1), (right, half, 3)):
             piece = wfull.at[u, xx, c]
             drain(piece, wx_r.at[u, xx])
+            part_ = wfull.at[u, xx, c, pl.ds(start, half)]
+            remote(part_, part_, wx_s, wx_r.at[u, xx], xpeer(e))
             remote(piece, piece, wc_s, wc_r.at[u, xx], sibling)
 
-    def context_gradient(d):
-        u = (z + d) % NZ
-
+    def forward_last(u):
+        xx = (x + 2) % NX
+        piece = wfull.at[u, xx, c]
+        drain(piece, wx_r.at[u, xx])
+        remote(piece, piece, wc_s, wc_r.at[u, xx], sibling)
+
+    def context_gradient(u):
         def one_head(e, carry):
             xx = (x + e) % NX
             h = u * NX + xx
@@ -245,9 +259,10 @@
 
         lax.fori_loop(0, NX, one_head, 0)
 
-    forward_z(1)
-    forward_z(3)
-    forward_x(0)
+    forward_z(near, pair)
+    forward_x(mine)
+    forward_z(next_, outer)
+    forward_last(mine)
 
     drain(w_ref, own_sem)
     drain(ab.at[:, :, 0], abz_r.at[2])
@@ -255,18 +270,22 @@
     both = dot(cot[...], ab[...].reshape(MODEL_WIDTH, 2 * ADAPTER_RANK), 1, 0)
     d0[...] = jnp.where(lane < ADAPTER_RANK, pltpu.roll(both, ADAPTER_RANK, 1), 0.0).astype(BF16)
 
-    context_gradient(0)
-    forward_z(2)
-    forward_x(1)
-    forward_x(3)
-    context_gradient(1)
+    context_gradient(mine)
+    forward_x(near)
+    forward_z(far, None)
+    forward_last(near)
+    context_gradient(near)
+    forward_x(next_)
+    forward_last(next_)
+    context_gradient(next_)
+    forward_x(far)
 
     drain(kh, qkv_r.at[0])
     drain(qh, qkv_r.at[1])
     drain(vh, qkv_r.at[2])
 
     def gathered(ref, i):
-        return jnp.concatenate([ref[blk[0, i, s]] for s in range(KEY_BLOCKS)], axis=0)
+        return jnp.concatenate([ref[blk[s, 0, i]] for s in range(KEY_BLOCKS)], axis=0)
 
     def send_block(src, dst_ref, n, i):
         @pl.when(i != j)
@@ -290,11 +309,25 @@
         send_block(ctx_heads, ctx, 0, i)
         return carry
 
-    lax.fori_loop(1, NB + 1, forward_block, 0)
-
-    context_gradient(3)
-    forward_x(2)
-    context_gradient(2)
+    lax.fori_loop(1, NB + 1, forward_block, 0, unroll=2)
+
+    forward_last(far)
+    context_gradient(far)
+
+    drain(ctx, blk_r.at[0])
+    both = dot(ctx[...], ab[...].reshape(MODEL_WIDTH, 2 * ADAPTER_RANK), 1, 0)
+    low = jnp.where(lane >= ADAPTER_RANK, pltpu.roll(both, ADAPTER_RANK, 1), 0.0).astype(BF16)
+    l0[...] = low
+    normal = 1.0 / math.sqrt(TOKENS)
+
+    def partial(h, carry):
+        s = dot(ctx[:, cols(h)], d0[...], 0, 0) + dot(cot[:, cols(h)], l0[...], 0, 0)
+        part[h // NX, h % NX] = (s * normal).reshape(2, SHARD, BLOCK)
+        return carry
+
+    lax.fori_loop(0, HEADS, partial, 0, unroll=2)
+    remote(part.at[:, :, oc], rc, red_s.at[0], red_r.at[0], sibling)
+
     drain(gh, blk_r.at[1])
 
     def backward_block(t, carry):
@@ -308,7 +341,17 @@
         send_block(dqb, dq_ref, 2, i)
         return carry
 
-    lax.fori_loop(1, NB + 1, backward_block, 0)
+    lax.fori_loop(1, NB + 1, backward_block, 0, unroll=2)
+
+    drain(rc, red_r.at[0])
+
+    def add_core(u, carry):
+        s1[u] = part[u, :, c] + rc[u]
+        return carry
+
+    lax.fori_loop(0, NZ, add_core, 0)
+    for e in (1, 3, 2):
+        remote(s1.at[:, (x + e) % NX], rx.at[x], red_s.at[1], red_r.at[1], xpeer(e))
 
     def random_terms(p, carry):
         r = perm[p]
@@ -322,31 +365,28 @@
         return acc_k, acc_v
 
     zero = jnp.zeros((BLOCK, BLOCK), F32)
-    lax.fori_loop(0, RANDOM, random_terms, (zero, zero))
-
-    def common_terms(i, carry):
-        return (
-            carry[0] + dot(dsc[i, 3], qh[i], 1, 0),
-            carry[1] + dot(wts[i, 3], gh[i], 1, 0),
-        )
-
-    common_k, common_v = lax.fori_loop(0, NB, common_terms, (zero, zero))
-    pre_k[RANDOM] = common_k
-    pre_v[RANDOM] = common_v
-    common = blk[0, 0, 3]
+    lax.fori_loop(0, RANDOM, random_terms, (zero, zero), unroll=4)
+
+    def long_dot(terms, rows):
+        wide = jnp.concatenate(terms, axis=1)
+        return dot(wide, jnp.concatenate(rows, axis=0), 1, 0)
+
+    every = range(NB)
+    pre_k[RANDOM] = long_dot([dsc[i, 3] for i in every], [qh[i] for i in every])
+    pre_v[RANDOM] = long_dot([wts[i, 3] for i in every], [gh[i] for i in every])
+    common = blk[3, 0, 0]
 
     def key_block(t, carry):
         n = sp_peer(t)
         before, after = (n + NB - 1) % NB, (n + 1) % NB
-        slot_before = jnp.where(blk[0, before, 2] == n, 2, 0)
-        slot_after = jnp.where(blk[0, after, 0] == n, 0, 2)
+        slot_before = jnp.where(blk[2, 0, before] == n, 2, 0)
+        slot_after = jnp.where(blk[0, 0, after] == n, 0, 2)
         is_common = jnp.where(common == n, 1.0, 0.0).astype(F32)
 
         def total(terms, rows, pre):
-            window = (
-                dot(terms[n, 1], rows[n], 1, 0)
-                + dot(terms[before, slot_before], rows[before], 1, 0)
-                + dot(terms[after, slot_after], rows[after], 1, 0)
+            window = long_dot(
+                [terms[n, 1], terms[before, slot_before], terms[after, slot_after]],
+                [rows[n], rows[before], rows[after]],
             )
             return (window + pre[last[n]] * has[n] + pre[RANDOM] * is_common).astype(BF16)
 
@@ -358,43 +398,22 @@
 
     lax.fori_loop(1, NB + 1, key_block, 0)
 
-    drain(ctx, blk_r.at[0])
-    both = dot(ctx[...], ab[...].reshape(MODEL_WIDTH, 2 * ADAPTER_RANK), 1, 0)
-    low = jnp.where(lane >= ADAPTER_RANK, pltpu.roll(both, ADAPTER_RANK, 1), 0.0).astype(BF16)
-    normal = 1.0 / math.sqrt(TOKENS)
-
-    def partial(h, carry):
-        s = dot(ctx[:, cols(h)], d0[...], 0, 0) + dot(cot[:, cols(h)], low, 0, 0)
-        part[h // NX, h % NX] = (s * normal).reshape(2, SHARD, BLOCK)
-        return carry
-
-    lax.fori_loop(0, HEADS, partial, 0)
-    remote(part.at[:, :, oc], rc, red_s.at[0], red_r.at[0], sibling)
-
-    wide = 256
-
-    def output_columns(n, carry):
-        rows = wfull[:, :, :, :, pl.ds(pl.multiple_of(n * wide, wide), wide)]
-        adapter = ab[n // 2, pl.ds(2 * (n % 2), 2)].reshape(wide, 2 * ADAPTER_RANK)
-        m = dot(ctx[...], rows.reshape(MODEL_WIDTH, wide), 1, 0) + dot(low, adapter, 1, 1)
-        mixed_ref[:, pl.ds(pl.multiple_of(n * wide, wide), wide)] = m.astype(BF16)
-        return carry
-
-    lax.fori_loop(0, MODEL_WIDTH // wide, output_columns, 0)
-
-    drain(rc, red_r.at[0])
-
-    def add_core(u, carry):
-        s1[u] = part[u, :, c] + rc[u]
-        return carry
-
-    lax.fori_loop(0, NZ, add_core, 0)
-    for e in (1, 3, 2):
-        remote(s1.at[:, (x + e) % NX], rx.at[x], red_s.at[1], red_r.at[1], xpeer(e))
     drain(rx.at[pl.ds(0, 3)], red_r.at[1])
     s2[...] = s1[:, x] + rx[(x + 1) % NX] + rx[(x + 2) % NX] + rx[(x + 3) % NX]
     for e in (1, 3, 2):
         remote(s2.at[(z + e) % NZ], rz.at[z], red_s.at[2], red_r.at[2], zpeer(e))
+
+    wide = 256
+
+    def output_columns(n, carry):
+        rows = wfull[:, :, :, :, pl.ds(pl.multiple_of(n * wide, wide), wide)]
+        adapter = ab[n // 2, pl.ds(2 * (n % 2), 2)].reshape(wide, 2 * ADAPTER_RANK)
+        m = dot(ctx[...], rows.reshape(MODEL_WIDTH, wide), 1, 0) + dot(l0[...], adapter, 1, 1)
+        mixed_ref[:, pl.ds(pl.multiple_of(n * wide, wide), wide)] = m.astype(BF16)
+        return carry
+
+    lax.fori_loop(0, MODEL_WIDTH // wide, output_columns, 0)
+
     drain(rz.at[pl.ds(0, 3)], red_r.at[2])
     s3[...] = s2[z] + rz[(z + 1) % NZ] + rz[(z + 2) % NZ] + rz[(z + 3) % NZ]
     remote(s3, rl, red_s.at[3], red_r.at[3], (f, (1 - zl) * NY + y))
@@ -438,6 +457,12 @@
     drain(ry.at[pl.ds(0, NY - 1)], red_s.at[5])
 
 
+def copy_out(*refs):
+    n = len(refs) // 2
+    for source, target in zip(refs[:n], refs[n:]):
+        target[...] = source[...]
+
+
 def shards(q, k, v, blocks, w, a, b, cot):
     hbm = pl.BlockSpec(memory_space=pl.ANY)
     vmem = pl.BlockSpec(memory_space=pltpu.VMEM)
@@ -446,7 +471,7 @@
     blocks3 = pltpu.VMEM((NB, BLOCK, BLOCK), BF16)
     tokens = jax.ShapeDtypeStruct((BLOCK, MODEL_WIDTH), BF16)
     grad = jax.ShapeDtypeStruct((SHARD, ADAPTER_RANK), F32)
-    return pl.pallas_call(
+    outs = pl.pallas_call(
         kernel,
         out_shape=(tokens, tokens, tokens, tokens, grad, grad),
         in_specs=[hbm, hbm, hbm, smem, hbm, vmem, vmem, vmem],
@@ -469,6 +494,7 @@
             pltpu.VMEM((NB, KEY_BLOCKS, BLOCK, BLOCK), BF16),
             pltpu.VMEM((RANDOM + 1, BLOCK, BLOCK), F32),
             pltpu.VMEM((RANDOM + 1, BLOCK, BLOCK), F32),
+            pltpu.VMEM((BLOCK, 2 * ADAPTER_RANK), BF16),
             pltpu.VMEM((BLOCK, 2 * ADAPTER_RANK), BF16),
             pltpu.VMEM((NZ, NX, 2, SHARD, BLOCK), F32),
             pltpu.VMEM((NZ, NX, SHARD, BLOCK), F32),
@@ -506,7 +532,16 @@
         compiler_params=pltpu.CompilerParams(
             collective_id=0, has_side_effects=True, vmem_limit_bytes=60 * 2**20
         ),
-    )(q, k, v, blocks, w, a, b, cot)
+    )(q, k, v, jnp.transpose(blocks, (2, 0, 1)), w, a, b, cot)
+    steps = 4
+    pieces = [pl.BlockSpec((o.shape[0] // steps, o.shape[1]), lambda i: (i, 0)) for o in outs]
+    return pl.pallas_call(
+        copy_out,
+        out_shape=tuple(jax.ShapeDtypeStruct(o.shape, o.dtype) for o in outs),
+        grid=(steps,),
+        in_specs=pieces,
+        out_specs=tuple(pieces),
+    )(*outs)
 
 
 def solution(mesh):

time: 161 us -> 131 us (0.81)
  the two profiles are of different devices: /device:TPU:6 before, /device:TPU:1 now
where the time goes in v2:
time: 131 us
  Pallas kernels  130 us (99%)
    pallas_call x1, Pallas kernels, shards(): pl.pallas_call(kernel, out_shape=(tokens, tokens, tokens, tokens, grad, g...  127 us
    pallas_call x1, Pallas kernels, shards(): pl.pallas_call(copy_out, out_shape=tuple((jax.ShapeDtypeStruct(o.shape, o...  3.84 us

profile of v2, /device:TPU:1, one launch (start us, length us, event | category | flops | bytes accessed | tf_op | source)
XLA Modules:
  0.0 131.1 jit_solution(6365743156655215987)
XLA Ops:
  0.6 126.6 %shard_map.127 = (bf16[128,2048]{1,0:T(8,128)(2,1)}, bf16[128,2048]{1,0:T(8,128)(2,1)}, bf16[128,2048]{1,0:T(8,128)(2,1)}, bf16[128,2048]{1,0:T(8,128)(2,1)}, f32[64,64]{1,0:T(8,128)}, /*index=5*/f32[64,64]{1,0:T(8,128)}) custom-call(bf16[128,2048]{1,0:T(8,128)(2,1)} %q_ref.1, bf16[128,2048]{1,0:T(8,128)(2,1)} %k_ref.1, bf16[128,2048]{1,0:T(8,128)(2,1)} %v_ref.1, ...), custom_call_target="tpu_custom_call" | custom-call | tf_op jit(solution)/shard_map/pallas_call | solution.py:474
  127.3 3.8 %shard_map.128 = (bf16[128,2048]{1,0:T(8,128)(2,1)}, bf16[128,2048]{1,0:T(8,128)(2,1)}, bf16[128,2048]{1,0:T(8,128)(2,1)}, bf16[128,2048]{1,0:T(8,128)(2,1)}, f32[64,64]{1,0:T(8,128)}, /*index=5*/f32[64,64]{1,0:T(8,128)}) custom-call(bf16[128,2048]{1,0:T(8,128)(2,1)} %get-tuple-element.12.refs_0_, bf16[128,2048]{1,0:T(8,128)(2,1)} %get-tuple-element.13.refs_1_, ...), custom_call_target="tpu_custom_call" | custom-call | tf_op jit(solution)/shard_map/pallas_call | solution.py:538

commit v3 on v2

--- a/solution.py
+++ b/solution.py
@@ -114,6 +114,11 @@
     def sp_peer(d):
         return (j + d) % NB
 
+    def peer(t):
+        k = t // NL
+        away = NY // 2 + (1 - 2 * (k % 2)) * ((k + 1) // 2)
+        return ((zl + t % NL) % NL) * NY + (y + away) % NY
+
     sibling = (fid(z, x, oc), j)
 
     def xpeer(d):
@@ -154,12 +159,12 @@
 
     for n, (src, dst) in enumerate(((k_ref, kh), (q_ref, qh), (v_ref, vh))):
 
-        def send_heads(d, carry, src=src, dst=dst, n=n):
-            h = sp_peer(d)
+        def send_heads(t, carry, src=src, dst=dst, n=n):
+            h = peer(t + t // (NB - 2))
             remote(src.at[:, cols(h)], dst.at[j], qkv_s.at[n], qkv_r.at[n], (f, h))
             return carry
 
-        lax.fori_loop(1, NB, send_heads, 0)
+        lax.fori_loop(0, NB - 1, send_heads, 0)
         pltpu.make_async_copy(src.at[:, cols(j)], dst.at[j], qkv_r.at[n]).start()
         if n == 0:
             remote(w_ref, wfull.at[z, x, c], wz_s, wz_r.at[z], outer)
@@ -237,28 +242,6 @@
         drain(piece, wx_r.at[u, xx])
         remote(piece, piece, wc_s, wc_r.at[u, xx], sibling)
 
-    def context_gradient(u):
-        def one_head(e, carry):
-            xx = (x + e) % NX
-            h = u * NX + xx
-            drain(wfull.at[u, xx, oc], wc_r.at[u, xx])
-            rows = wfull[u, xx].reshape(BLOCK, MODEL_WIDTH)
-            adapter = ab[u, xx].reshape(BLOCK, 2 * ADAPTER_RANK)
-            g = dot(cot[...], rows, 1, 1) + dot(d0[...], adapter, 1, 1)
-            dctx_send[h] = g.astype(BF16)
-
-            @pl.when(h != j)
-            def _():
-                remote(dctx_send.at[h], gh.at[j], blk_s.at[1], blk_r.at[1], (f, h))
-
-            @pl.when(h == j)
-            def _():
-                pltpu.make_async_copy(dctx_send.at[h], gh.at[j], blk_r.at[1]).start()
-
-            return carry
-
-        lax.fori_loop(0, NX, one_head, 0)
-
     forward_z(near, pair)
     forward_x(mine)
     forward_z(next_, outer)
@@ -270,14 +253,11 @@
     both = dot(cot[...], ab[...].reshape(MODEL_WIDTH, 2 * ADAPTER_RANK), 1, 0)
     d0[...] = jnp.where(lane < ADAPTER_RANK, pltpu.roll(both, ADAPTER_RANK, 1), 0.0).astype(BF16)
 
-    context_gradient(mine)
     forward_x(near)
     forward_z(far, None)
     forward_last(near)
-    context_gradient(near)
     forward_x(next_)
     forward_last(next_)
-    context_gradient(next_)
     forward_x(far)
 
     drain(kh, qkv_r.at[0])
@@ -297,7 +277,7 @@
             pltpu.make_async_copy(src.at[i], dst_ref.at[:, cols(j)], blk_r.at[n]).start()
 
     def forward_block(t, carry):
-        i = sp_peer(t)
+        i = peer(t)
         scores = dot(gathered(kh, i), qh[i], 1, 1)
         highest = jnp.max(scores, axis=0, keepdims=True)
         raised = jnp.exp2((scores - highest) * (scaling * log2e))
@@ -309,10 +289,30 @@
         send_block(ctx_heads, ctx, 0, i)
         return carry
 
-    lax.fori_loop(1, NB + 1, forward_block, 0, unroll=2)
+    lax.fori_loop(0, NB, forward_block, 0, unroll=2)
 
     forward_last(far)
-    context_gradient(far)
+
+    def context_gradient(t, carry):
+        h = peer(t)
+        u, xx = h // NX, h % NX
+        drain(wfull.at[u, xx, oc], wc_r.at[u, xx])
+        rows = wfull[u, xx].reshape(BLOCK, MODEL_WIDTH)
+        adapter = ab[u, xx].reshape(BLOCK, 2 * ADAPTER_RANK)
+        g = dot(cot[...], rows, 1, 1) + dot(d0[...], adapter, 1, 1)
+        dctx_send[h] = g.astype(BF16)
+
+        @pl.when(h != j)
+        def _():
+            remote(dctx_send.at[h], gh.at[j], blk_s.at[1], blk_r.at[1], (f, h))
+
+        @pl.when(h == j)
+        def _():
+            pltpu.make_async_copy(dctx_send.at[h], gh.at[j], blk_r.at[1]).start()
+
+        return carry
+
+    lax.fori_loop(0, NB, context_gradient, 0, unroll=2)
 
     drain(ctx, blk_r.at[0])
     both = dot(ctx[...], ab[...].reshape(MODEL_WIDTH, 2 * ADAPTER_RANK), 1, 0)
@@ -328,10 +328,20 @@
     lax.fori_loop(0, HEADS, partial, 0, unroll=2)
     remote(part.at[:, :, oc], rc, red_s.at[0], red_r.at[0], sibling)
 
+    drain(rc, red_r.at[0])
+
+    def add_core(u, carry):
+        s1[u] = part[u, :, c] + rc[u]
+        return carry
+
+    lax.fori_loop(0, NZ, add_core, 0)
+    for e in (1, 3, 2):
+        remote(s1.at[:, (x + e) % NX], rx.at[x], red_s.at[1], red_r.at[1], xpeer(e))
+
     drain(gh, blk_r.at[1])
 
     def backward_block(t, carry):
-        i = sp_peer(t)
+        i = peer(t)
         p = probs[i]
         dw = dot(gathered(vh, i), gh[i], 1, 1)
         correction = jnp.sum(p * dw, axis=0, keepdims=True)
@@ -341,67 +351,61 @@
         send_block(dqb, dq_ref, 2, i)
         return carry
 
-    lax.fori_loop(1, NB + 1, backward_block, 0, unroll=2)
-
-    drain(rc, red_r.at[0])
-
-    def add_core(u, carry):
-        s1[u] = part[u, :, c] + rc[u]
-        return carry
-
-    lax.fori_loop(0, NZ, add_core, 0)
+    lax.fori_loop(0, NB, backward_block, 0, unroll=2)
+
+    drain(rx.at[pl.ds(0, 3)], red_r.at[1])
+    s2[...] = s1[:, x] + rx[(x + 1) % NX] + rx[(x + 2) % NX] + rx[(x + 3) % NX]
     for e in (1, 3, 2):
-        remote(s1.at[:, (x + e) % NX], rx.at[x], red_s.at[1], red_r.at[1], xpeer(e))
-
-    def random_terms(p, carry):
-        r = perm[p]
-        i = r // 2
-        slot = 4 + r % 2
-        keep = same[p]
-        acc_k = carry[0] * keep + dot(dsc[i, slot], qh[i], 1, 0)
-        acc_v = carry[1] * keep + dot(wts[i, slot], gh[i], 1, 0)
-        pre_k[p] = acc_k
-        pre_v[p] = acc_v
-        return acc_k, acc_v
+        remote(s2.at[(z + e) % NZ], rz.at[z], red_s.at[2], red_r.at[2], zpeer(e))
 
     zero = jnp.zeros((BLOCK, BLOCK), F32)
-    lax.fori_loop(0, RANDOM, random_terms, (zero, zero), unroll=4)
+    common = blk[3, 0, 0]
 
     def long_dot(terms, rows):
         wide = jnp.concatenate(terms, axis=1)
         return dot(wide, jnp.concatenate(rows, axis=0), 1, 0)
 
-    every = range(NB)
-    pre_k[RANDOM] = long_dot([dsc[i, 3] for i in every], [qh[i] for i in every])
-    pre_v[RANDOM] = long_dot([wts[i, 3] for i in every], [gh[i] for i in every])
-    common = blk[3, 0, 0]
-
-    def key_block(t, carry):
-        n = sp_peer(t)
-        before, after = (n + NB - 1) % NB, (n + 1) % NB
-        slot_before = jnp.where(blk[2, 0, before] == n, 2, 0)
-        slot_after = jnp.where(blk[0, 0, after] == n, 0, 2)
-        is_common = jnp.where(common == n, 1.0, 0.0).astype(F32)
-
-        def total(terms, rows, pre):
+    def listed_terms(terms, rows, pre):
+        def random_terms(p, carry):
+            r = perm[p]
+            i = r // 2
+            slot = 4 + r % 2
+            acc = carry * same[p] + dot(terms[i, slot], rows[i], 1, 0)
+            pre[p] = acc
+            return acc
+
+        lax.fori_loop(0, RANDOM, random_terms, zero, unroll=4)
+        pre[RANDOM] = long_dot([terms[i, 3] for i in range(NB)], [rows[i] for i in range(NB)])
+
+    def key_blocks(terms, rows, pre, out, out_ref, slot):
+        def key_block(t, carry):
+            n = peer(t)
+            before, after = (n + NB - 1) % NB, (n + 1) % NB
+            slot_before = jnp.where(blk[2, 0, before] == n, 2, 0)
+            slot_after = jnp.where(blk[0, 0, after] == n, 0, 2)
+            is_common = jnp.where(common == n, 1.0, 0.0).astype(F32)
             window = long_dot(
                 [terms[n, 1], terms[before, slot_before], terms[after, slot_after]],
                 [rows[n], rows[before], rows[after]],
             )
-            return (window + pre[last[n]] * has[n] + pre[RANDOM] * is_common).astype(BF16)
-
-        dkb[n] = total(dsc, qh, pre_k)
-        send_block(dkb, dk_ref, 3, n)
-        dvb[n] = total(wts, gh, pre_v)
-        send_block(dvb, dv_ref, 4, n)
-        return carry
-
-    lax.fori_loop(1, NB + 1, key_block, 0)
-
-    drain(rx.at[pl.ds(0, 3)], red_r.at[1])
-    s2[...] = s1[:, x] + rx[(x + 1) % NX] + rx[(x + 2) % NX] + rx[(x + 3) % NX]
-    for e in (1, 3, 2):
-        remote(s2.at[(z + e) % NZ], rz.at[z], red_s.at[2], red_r.at[2], zpeer(e))
+            out[n] = (window + pre[last[n]] * has[n] + pre[RANDOM] * is_common).astype(BF16)
+            send_block(out, out_ref, slot, n)
+            return carry
+
+        lax.fori_loop(0, NB, key_block, 0, unroll=2)
+
+    listed_terms(wts, gh, pre_v)
+    drain(rz.at[pl.ds(0, 3)], red_r.at[2])
+    s3[...] = s2[z] + rz[(z + 1) % NZ] + rz[(z + 2) % NZ] + rz[(z + 3) % NZ]
+    remote(s3, rl, red_s.at[3], red_r.at[3], pair)
+    key_blocks(wts, gh, pre_v, dvb, dv_ref, 4)
+    listed_terms(dsc, qh, pre_k)
+    drain(rl, red_r.at[3])
+    s4[...] = (s3[...] + rl[...]).reshape(NY, 8, BLOCK)
+    for e in range(1, NY):
+        yy = (y + e) % NY
+        remote(s4.at[yy], ry.at[y], red_s.at[4], red_r.at[4], (f, zl * NY + yy))
+    key_blocks(dsc, qh, pre_k, dkb, dk_ref, 3)
 
     wide = 256
 
@@ -413,15 +417,6 @@
         return carry
 
     lax.fori_loop(0, MODEL_WIDTH // wide, output_columns, 0)
-
-    drain(rz.at[pl.ds(0, 3)], red_r.at[2])
-    s3[...] = s2[z] + rz[(z + 1) % NZ] + rz[(z + 2) % NZ] + rz[(z + 3) % NZ]
-    remote(s3, rl, red_s.at[3], red_r.at[3], (f, (1 - zl) * NY + y))
-    drain(rl, red_r.at[3])
-    s4[...] = (s3[...] + rl[...]).reshape(NY, 8, BLOCK)
-    for e in range(1, NY):
-        yy = (y + e) % NY
-        remote(s4.at[yy], ry.at[y], red_s.at[4], red_r.at[4], (f, zl * NY + yy))
     drain(ry.at[pl.ds(0, NY - 1)], red_r.at[4])
     total = s4[y]
     for e in range(1, NY):
@@ -431,6 +426,7 @@
     for e in range(1, NY):
         yy = (y + e) % NY
         remote(s5, gfin.at[y], red_s.at[5], red_r.at[5], (f, zl * NY + yy))
+
     drain(ry.at[pl.ds(0, NY - 1)], red_r.at[5])
     both = gfin[...].reshape(SHARD, BLOCK)
     gd_ref[...] = both[:, :ADAPTER_RANK]
@@ -458,9 +454,18 @@
 
 
 def copy_out(*refs):
-    n = len(refs) // 2
-    for source, target in zip(refs[:n], refs[n:]):
-        target[...] = source[...]
+    n = (len(refs) - 2) // 3
+    sources, targets, held = refs[:n], refs[n : 2 * n], refs[2 * n : 3 * n]
+    in_sem, out_sem = refs[3 * n :]
+    inward = [pltpu.make_async_copy(sources[i], held[i], in_sem.at[i]) for i in range(n)]
+    outward = [pltpu.make_async_copy(held[i], targets[i], out_sem.at[i]) for i in range(n)]
+    for copy in inward:
+        copy.start()
+    for i in range(n):
+        inward[i].wait()
+        outward[i].start()
+    for copy in outward:
+        copy.wait()
 
 
 def shards(q, k, v, blocks, w, a, b, cot):
@@ -533,14 +538,13 @@
             collective_id=0, has_side_effects=True, vmem_limit_bytes=60 * 2**20
         ),
     )(q, k, v, jnp.transpose(blocks, (2, 0, 1)), w, a, b, cot)
-    steps = 4
-    pieces = [pl.BlockSpec((o.shape[0] // steps, o.shape[1]), lambda i: (i, 0)) for o in outs]
     return pl.pallas_call(
         copy_out,
         out_shape=tuple(jax.ShapeDtypeStruct(o.shape, o.dtype) for o in outs),
-        grid=(steps,),
-        in_specs=pieces,
-        out_specs=tuple(pieces),
+        in_specs=[hbm] * len(outs),
+        out_specs=(hbm,) * len(outs),
+        scratch_shapes=[pltpu.VMEM(o.shape, o.dtype) for o in outs] + [dma((len(outs),)), dma((len(outs),))],
+        compiler_params=pltpu.CompilerParams(vmem_limit_bytes=60 * 2**20),
     )(*outs)
 
 

time: 131 us -> 132 us (level)
    pallas_call x1, Pallas kernels: 127 us -> 129 us  [shards(): pl.pallas_call(kernel, out_shape=(tokens, tokens, tokens, tokens, grad, g...]
    pallas_call x1, Pallas kernels: 3.84 us -> 2.46 us  [shards(): pl.pallas_call(copy_out, out_shape=tuple((jax.ShapeDtypeStruct(o.shape, o...]
where the time goes in v3:
time: 132 us
  Pallas kernels  131 us (99%)
    pallas_call x1, Pallas kernels, shards(): pl.pallas_call(kernel, out_shape=(tokens, tokens, tokens, tokens, grad, g...  129 us

profile of v3, /device:TPU:1, one launch (start us, length us, event | category | flops | bytes accessed | tf_op | source)
XLA Modules:
  0.0 131.7 jit_solution(10370322210473232561)
XLA Ops:
  0.6 128.6 %shard_map.127 = (bf16[128,2048]{1,0:T(8,128)(2,1)}, bf16[128,2048]{1,0:T(8,128)(2,1)}, bf16[128,2048]{1,0:T(8,128)(2,1)}, bf16[128,2048]{1,0:T(8,128)(2,1)}, f32[64,64]{1,0:T(8,128)}, /*index=5*/f32[64,64]{1,0:T(8,128)}) custom-call(bf16[128,2048]{1,0:T(8,128)(2,1)} %q_ref.1, bf16[128,2048]{1,0:T(8,128)(2,1)} %k_ref.1, bf16[128,2048]{1,0:T(8,128)(2,1)} %v_ref.1, ...), custom_call_target="tpu_custom_call" | custom-call | tf_op jit(solution)/shard_map/pallas_call | solution.py:479
  129.2 2.5 %shard_map.128 = (bf16[128,2048]{1,0:T(8,128)(2,1)}, bf16[128,2048]{1,0:T(8,128)(2,1)}, bf16[128,2048]{1,0:T(8,128)(2,1)}, bf16[128,2048]{1,0:T(8,128)(2,1)}, f32[64,64]{1,0:T(8,128)}, /*index=5*/f32[64,64]{1,0:T(8,128)}) custom-call(bf16[128,2048]{1,0:T(8,128)(2,1)} %get-tuple-element.12.refs_0_, bf16[128,2048]{1,0:T(8,128)(2,1)} %get-tuple-element.13.refs_1_, ...), custom_call_target="tpu_custom_call" | custom-call | tf_op jit(solution)/shard_map/pallas_call | solution.py:541

commit v4 on v2

--- a/solution.py
+++ b/solution.py
@@ -114,6 +114,11 @@
     def sp_peer(d):
         return (j + d) % NB
 
+    def peer(t):
+        k = t // NL
+        away = NY // 2 + (1 - 2 * (k % 2)) * ((k + 1) // 2)
+        return ((zl + t % NL) % NL) * NY + (y + away) % NY
+
     sibling = (fid(z, x, oc), j)
 
     def xpeer(d):
@@ -154,12 +159,12 @@
 
     for n, (src, dst) in enumerate(((k_ref, kh), (q_ref, qh), (v_ref, vh))):
 
-        def send_heads(d, carry, src=src, dst=dst, n=n):
-            h = sp_peer(d)
+        def send_heads(t, carry, src=src, dst=dst, n=n):
+            h = peer(t + t // (NB - 2))
             remote(src.at[:, cols(h)], dst.at[j], qkv_s.at[n], qkv_r.at[n], (f, h))
             return carry
 
-        lax.fori_loop(1, NB, send_heads, 0)
+        lax.fori_loop(0, NB - 1, send_heads, 0)
         pltpu.make_async_copy(src.at[:, cols(j)], dst.at[j], qkv_r.at[n]).start()
         if n == 0:
             remote(w_ref, wfull.at[z, x, c], wz_s, wz_r.at[z], outer)
@@ -297,7 +302,7 @@
             pltpu.make_async_copy(src.at[i], dst_ref.at[:, cols(j)], blk_r.at[n]).start()
 
     def forward_block(t, carry):
-        i = sp_peer(t)
+        i = peer(t)
         scores = dot(gathered(kh, i), qh[i], 1, 1)
         highest = jnp.max(scores, axis=0, keepdims=True)
         raised = jnp.exp2((scores - highest) * (scaling * log2e))
@@ -309,9 +314,10 @@
         send_block(ctx_heads, ctx, 0, i)
         return carry
 
-    lax.fori_loop(1, NB + 1, forward_block, 0, unroll=2)
+    lax.fori_loop(0, NB, forward_block, 0, unroll=2)
 
     forward_last(far)
+
     context_gradient(far)
 
     drain(ctx, blk_r.at[0])
@@ -331,7 +337,7 @@
     drain(gh, blk_r.at[1])
 
     def backward_block(t, carry):
-        i = sp_peer(t)
+        i = peer(t)
         p = probs[i]
         dw = dot(gathered(vh, i), gh[i], 1, 1)
         correction = jnp.sum(p * dw, axis=0, keepdims=True)
@@ -341,7 +347,7 @@
         send_block(dqb, dq_ref, 2, i)
         return carry
 
-    lax.fori_loop(1, NB + 1, backward_block, 0, unroll=2)
+    lax.fori_loop(0, NB, backward_block, 0, unroll=2)
 
     drain(rc, red_r.at[0])
 
@@ -377,7 +383,7 @@
     common = blk[3, 0, 0]
 
     def key_block(t, carry):
-        n = sp_peer(t)
+        n = peer(t)
         before, after = (n + NB - 1) % NB, (n + 1) % NB
         slot_before = jnp.where(blk[2, 0, before] == n, 2, 0)
         slot_after = jnp.where(blk[0, 0, after] == n, 0, 2)
@@ -396,7 +402,7 @@
         send_block(dvb, dv_ref, 4, n)
         return carry
 
-    lax.fori_loop(1, NB + 1, key_block, 0)
+    lax.fori_loop(0, NB, key_block, 0)
 
     drain(rx.at[pl.ds(0, 3)], red_r.at[1])
     s2[...] = s1[:, x] + rx[(x + 1) % NX] + rx[(x + 2) % NX] + rx[(x + 3) % NX]
@@ -458,9 +464,18 @@
 
 
 def copy_out(*refs):
-    n = len(refs) // 2
-    for source, target in zip(refs[:n], refs[n:]):
-        target[...] = source[...]
+    n = (len(refs) - 2) // 3
+    sources, targets, held = refs[:n], refs[n : 2 * n], refs[2 * n : 3 * n]
+    in_sem, out_sem = refs[3 * n :]
+    inward = [pltpu.make_async_copy(sources[i], held[i], in_sem.at[i]) for i in range(n)]
+    outward = [pltpu.make_async_copy(held[i], targets[i], out_sem.at[i]) for i in range(n)]
+    for copy in inward:
+        copy.start()
+    for i in range(n):
+        inward[i].wait()
+        outward[i].start()
+    for copy in outward:
+        copy.wait()
 
 
 def shards(q, k, v, blocks, w, a, b, cot):
@@ -533,14 +548,13 @@
             collective_id=0, has_side_effects=True, vmem_limit_bytes=60 * 2**20
         ),
     )(q, k, v, jnp.transpose(blocks, (2, 0, 1)), w, a, b, cot)
-    steps = 4
-    pieces = [pl.BlockSpec((o.shape[0] // steps, o.shape[1]), lambda i: (i, 0)) for o in outs]
     return pl.pallas_call(
         copy_out,
         out_shape=tuple(jax.ShapeDtypeStruct(o.shape, o.dtype) for o in outs),
-        grid=(steps,),
-        in_specs=pieces,
-        out_specs=tuple(pieces),
+        in_specs=[hbm] * len(outs),
+        out_specs=(hbm,) * len(outs),
+        scratch_shapes=[pltpu.VMEM(o.shape, o.dtype) for o in outs] + [dma((len(outs),)), dma((len(outs),))],
+        compiler_params=pltpu.CompilerParams(vmem_limit_bytes=60 * 2**20),
     )(*outs)
 
 

time: 131 us -> 129 us (0.985)
  the two profiles are of different devices: /device:TPU:1 before, /device:TPU:64 now
where the time goes in v4:
time: 129 us; the launch traced here: 128 us
  Pallas kernels  128 us (99%)
    pallas_call x1, Pallas kernels, shards(): pl.pallas_call(kernel, out_shape=(tokens, tokens, tokens, tokens, grad, g...  125 us

profile of v4, /device:TPU:64, one launch (start us, length us, event | category | flops | bytes accessed | tf_op | source)
XLA Modules:
  0.0 128.4 jit_solution(14122739625959600025)
XLA Ops:
  0.6 125.3 %shard_map.127 = (bf16[128,2048]{1,0:T(8,128)(2,1)}, bf16[128,2048]{1,0:T(8,128)(2,1)}, bf16[128,2048]{1,0:T(8,128)(2,1)}, bf16[128,2048]{1,0:T(8,128)(2,1)}, f32[64,64]{1,0:T(8,128)}, /*index=5*/f32[64,64]{1,0:T(8,128)}) custom-call(bf16[128,2048]{1,0:T(8,128)(2,1)} %q_ref.1, bf16[128,2048]{1,0:T(8,128)(2,1)} %k_ref.1, bf16[128,2048]{1,0:T(8,128)(2,1)} %v_ref.1, ...), custom_call_target="tpu_custom_call" | custom-call | tf_op jit(solution)/shard_map/pallas_call | solution.py:489
  125.9 2.5 %shard_map.128 = (bf16[128,2048]{1,0:T(8,128)(2,1)}, bf16[128,2048]{1,0:T(8,128)(2,1)}, bf16[128,2048]{1,0:T(8,128)(2,1)}, bf16[128,2048]{1,0:T(8,128)(2,1)}, f32[64,64]{1,0:T(8,128)}, /*index=5*/f32[64,64]{1,0:T(8,128)}) custom-call(bf16[128,2048]{1,0:T(8,128)(2,1)} %get-tuple-element.12.refs_0_, bf16[128,2048]{1,0:T(8,128)(2,1)} %get-tuple-element.13.refs_1_, ...), custom_call_target="tpu_custom_call" | custom-call | tf_op jit(solution)/shard_map/pallas_call | solution.py:551

commit v5 on v4

--- a/solution.py
+++ b/solution.py
@@ -97,6 +97,7 @@
     wc_s,
     wc_r,
     own_sem,
+    gh_r,
     red_s,
     red_r,
 ):
@@ -242,28 +243,6 @@
         drain(piece, wx_r.at[u, xx])
         remote(piece, piece, wc_s, wc_r.at[u, xx], sibling)
 
-    def context_gradient(u):
-        def one_head(e, carry):
-            xx = (x + e) % NX
-            h = u * NX + xx
-            drain(wfull.at[u, xx, oc], wc_r.at[u, xx])
-            rows = wfull[u, xx].reshape(BLOCK, MODEL_WIDTH)
-            adapter = ab[u, xx].reshape(BLOCK, 2 * ADAPTER_RANK)
-            g = dot(cot[...], rows, 1, 1) + dot(d0[...], adapter, 1, 1)
-            dctx_send[h] = g.astype(BF16)
-
-            @pl.when(h != j)
-            def _():
-                remote(dctx_send.at[h], gh.at[j], blk_s.at[1], blk_r.at[1], (f, h))
-
-            @pl.when(h == j)
-            def _():
-                pltpu.make_async_copy(dctx_send.at[h], gh.at[j], blk_r.at[1]).start()
-
-            return carry
-
-        lax.fori_loop(0, NX, one_head, 0)
-
     forward_z(near, pair)
     forward_x(mine)
     forward_z(next_, outer)
@@ -275,14 +254,11 @@
     both = dot(cot[...], ab[...].reshape(MODEL_WIDTH, 2 * ADAPTER_RANK), 1, 0)
     d0[...] = jnp.where(lane < ADAPTER_RANK, pltpu.roll(both, ADAPTER_RANK, 1), 0.0).astype(BF16)
 
-    context_gradient(mine)
     forward_x(near)
     forward_z(far, None)
     forward_last(near)
-    context_gradient(near)
     forward_x(next_)
     forward_last(next_)
-    context_gradient(next_)
     forward_x(far)
 
     drain(kh, qkv_r.at[0])
@@ -318,7 +294,26 @@
 
     forward_last(far)
 
-    context_gradient(far)
+    def context_gradient(t, carry):
+        h = peer(t)
+        u, xx = h // NX, h % NX
+        drain(wfull.at[u, xx, oc], wc_r.at[u, xx])
+        rows = wfull[u, xx].reshape(BLOCK, MODEL_WIDTH)
+        adapter = ab[u, xx].reshape(BLOCK, 2 * ADAPTER_RANK)
+        g = dot(cot[...], rows, 1, 1) + dot(d0[...], adapter, 1, 1)
+        dctx_send[h] = g.astype(BF16)
+
+        @pl.when(h != j)
+        def _():
+            remote(dctx_send.at[h], gh.at[j], blk_s.at[1], gh_r.at[j], (f, h))
+
+        @pl.when(h == j)
+        def _():
+            pltpu.make_async_copy(dctx_send.at[h], gh.at[j], gh_r.at[j]).start()
+
+        return carry
+
+    lax.fori_loop(0, NB, context_gradient, 0, unroll=2)
 
     drain(ctx, blk_r.at[0])
     both = dot(ctx[...], ab[...].reshape(MODEL_WIDTH, 2 * ADAPTER_RANK), 1, 0)
@@ -334,10 +329,9 @@
     lax.fori_loop(0, HEADS, partial, 0, unroll=2)
     remote(part.at[:, :, oc], rc, red_s.at[0], red_r.at[0], sibling)
 
-    drain(gh, blk_r.at[1])
-
     def backward_block(t, carry):
         i = peer(t)
+        drain(gh.at[i], gh_r.at[i])
         p = probs[i]
         dw = dot(gathered(vh, i), gh[i], 1, 1)
         correction = jnp.sum(p * dw, axis=0, keepdims=True)
@@ -371,7 +365,7 @@
         return acc_k, acc_v
 
     zero = jnp.zeros((BLOCK, BLOCK), F32)
-    lax.fori_loop(0, RANDOM, random_terms, (zero, zero), unroll=4)
+    lax.fori_loop(0, RANDOM, random_terms, (zero, zero), unroll=8)
 
     def long_dot(terms, rows):
         wide = jnp.concatenate(terms, axis=1)
@@ -541,6 +535,7 @@
             dma,
             dma((NZ, NX)),
             dma,
+            dma((NB,)),
             dma((6,)),
             dma((6,)),
         ],

time: 129 us -> 126 us (0.977)
  the two profiles are of different devices: /device:TPU:64 before, /device:TPU:1 now
where the time goes in v5:
time: 126 us; the launch traced here: 125 us
  Pallas kernels  125 us (99%)
    pallas_call x1, Pallas kernels, shards(): pl.pallas_call(kernel, out_shape=(tokens, tokens, tokens, tokens, grad, g...  122 us

profile of v5, /device:TPU:1, one launch (start us, length us, event | category | flops | bytes accessed | tf_op | source)
XLA Modules:
  0.0 125.4 jit_solution(6478463765702981691)
XLA Ops:
  0.6 122.3 %shard_map.127 = (bf16[128,2048]{1,0:T(8,128)(2,1)}, bf16[128,2048]{1,0:T(8,128)(2,1)}, bf16[128,2048]{1,0:T(8,128)(2,1)}, bf16[128,2048]{1,0:T(8,128)(2,1)}, f32[64,64]{1,0:T(8,128)}, /*index=5*/f32[64,64]{1,0:T(8,128)}) custom-call(bf16[128,2048]{1,0:T(8,128)(2,1)} %q_ref.1, bf16[128,2048]{1,0:T(8,128)(2,1)} %k_ref.1, bf16[128,2048]{1,0:T(8,128)(2,1)} %v_ref.1, ...), custom_call_target="tpu_custom_call" | custom-call | tf_op jit(solution)/shard_map/pallas_call | solution.py:483
  123.0 2.5 %shard_map.128 = (bf16[128,2048]{1,0:T(8,128)(2,1)}, bf16[128,2048]{1,0:T(8,128)(2,1)}, bf16[128,2048]{1,0:T(8,128)(2,1)}, bf16[128,2048]{1,0:T(8,128)(2,1)}, f32[64,64]{1,0:T(8,128)}, /*index=5*/f32[64,64]{1,0:T(8,128)}) custom-call(bf16[128,2048]{1,0:T(8,128)(2,1)} %get-tuple-element.12.refs_0_, bf16[128,2048]{1,0:T(8,128)(2,1)} %get-tuple-element.13.refs_1_, ...), custom_call_target="tpu_custom_call" | custom-call | tf_op jit(solution)/shard_map/pallas_call | solution.py:546
